TPU v7x, 128 devices: a whole 4x4x4 slice. The times are simulated.
128 devices in a mesh: row: 16 (over x, z_lo, core), col: 8 (over y, z_hi).
Axes of the slice: x: 4, y: 4, z: 4 (z_hi: 2, z_lo: 2; z = z_hi * 2 + z_lo), core: 2. Of those that a mesh axis runs over, the one named last changes fastest.
Arguments:
- query_first: bfloat16 [3072, 8192], P('row', 'col'), may hold values from -180 to 180
- query_second: bfloat16 [3072, 8192], P('row', 'col'), may hold values from -180 to 180
- shared_key_states: bfloat16 [3072, 512], P('col', 'row'), may hold values from -7 to 7
- shared_value_states: bfloat16 [3072, 512], P('col', 'row'), may hold values from -6 to 6
- upstream_first: bfloat16 [3072, 8192], P('row', 'col'), may hold values from -6 to 6
- upstream_second: bfloat16 [3072, 8192], P('row', 'col'), may hold values from -6 to 6
- output_first: bfloat16 [3072, 8192], P('row', 'col'), may hold values from -6 to 6
- output_second: bfloat16 [3072, 8192], P('row', 'col'), may hold values from -6 to 6
- block_order: int32 [48], replicated, may hold values from 0 to 47, each once
Outputs:
- gradient_first: bfloat16 [3072, 8192], P('row', 'col')
- gradient_second: bfloat16 [3072, 8192], P('row', 'col')
- shared_key_gradient: bfloat16 [3072, 512], P('col', 'row')
- shared_value_gradient: bfloat16 [3072, 512], P('col', 'row')
Inputs may be any that keep to these rules, and one draw needn't show every extreme that they name: A permutation of the 48 sequence blocks: storage block j holds the positions block_order[j] * 64 to block_order[j] * 64 + 63 in order.
All inputs are finite; a program needn't handle non-finite values.
Results may differ from a plain program's by a relative error of at most 0.0056.
Values may be sent and summed in bfloat16 or wider, within the bound.
No kernel may reach another device: no remote copies, remote signals or barrier semaphores. Data moves between devices by JAX's collectives and lax.ppermute only.
A program may use at most 192 MiB of HBM per device.

v0:
```python
import math

import jax
import jax.numpy as jnp
from jax import lax
from jax.sharding import PartitionSpec as P

QUERY_HEADS = 64
SHARED_HEADS = 4
HEAD_SIZE = 128
BLK = 64


NEG = -1e30


def merged_2(value, axis, combine):
    everything = jax.tree.map(lambda part: lax.all_gather(part, axis), value)
    first = jax.tree.map(lambda part: part[0], everything)

    def lap(k, so_far):
        return combine(so_far, jax.tree.map(lambda part: part[k], everything))

    return lax.fori_loop(1, lax.axis_size(axis), lap, first)


def head_scores(query_group, key_group):
    return jnp.einsum("ihd,kd->hik", query_group, key_group, preferred_element_type=jnp.float32) * (
        1.0 / math.sqrt(HEAD_SIZE)
    )


def merge_stats(left_stats, right_stats):
    merged = []
    for layer_index in range(2):
        peak_left, total_left, delta_left = left_stats[3 * layer_index : 3 * layer_index + 3]
        peak_right, total_right, delta_right = right_stats[3 * layer_index : 3 * layer_index + 3]
        row_peak = jnp.maximum(peak_left, peak_right)
        row_total = total_left * jnp.exp(peak_left - row_peak) + total_right * jnp.exp(
            peak_right - row_peak
        )
        merged += [row_peak, row_total, delta_left + delta_right]
    return tuple(merged)


def grid_layout(arrays, key_full, value_full, allowed, col_index):
    query_first, query_second, upstream_first, upstream_second, output_first, output_second = arrays
    score_scale = 1.0 / math.sqrt(HEAD_SIZE)
    query_rows = query_first.shape[0]
    own_heads = query_first.shape[1] // HEAD_SIZE
    heads_per_group = QUERY_HEADS // SHARED_HEADS
    gathered = (
        lax.all_gather(query_first, "col", axis=1, tiled=True),
        lax.all_gather(query_second, "col", axis=1, tiled=True),
        lax.all_gather(upstream_first, "col", axis=1, tiled=True),
        lax.all_gather(upstream_second, "col", axis=1, tiled=True),
    )
    layers = (
        (query_first, upstream_first, output_first, gathered[0], gathered[2]),
        (query_second, upstream_second, output_second, gathered[1], gathered[3]),
    )
    own_deltas = []
    stat_terms = []
    saved_scores = []
    for own_query, upstream_own, output_own, query_all, upstream_all in layers:
        own_delta = jnp.sum(
            upstream_own.astype(jnp.float32).reshape(query_rows, own_heads, HEAD_SIZE)
            * output_own.astype(jnp.float32).reshape(query_rows, own_heads, HEAD_SIZE),
            axis=2,
        ).T
        own_deltas.append(own_delta)
        placed = lax.dynamic_update_slice_in_dim(
            jnp.zeros((QUERY_HEADS, query_rows), jnp.float32), own_delta, col_index * own_heads, 0
        )
        layer_scores = []
        peaks = []
        totals = []
        for grouped_heads in range(SHARED_HEADS):
            query_group = query_all[
                :,
                grouped_heads
                * heads_per_group
                * HEAD_SIZE : (grouped_heads + 1)
                * heads_per_group
                * HEAD_SIZE,
            ].reshape(query_rows, heads_per_group, HEAD_SIZE)
            key_group = key_full[:, grouped_heads * HEAD_SIZE : (grouped_heads + 1) * HEAD_SIZE]
            scores = head_scores(query_group, key_group)
            masked = jnp.where(allowed[None], scores, NEG)
            row_peak = jnp.max(masked, axis=2)
            row_total = jnp.sum(
                jnp.where(allowed[None], jnp.exp(masked - row_peak[:, :, None]), 0.0), axis=2
            )
            layer_scores.append(scores)
            peaks.append(row_peak)
            totals.append(row_total)
        stat_terms += [jnp.concatenate(peaks, axis=0), jnp.concatenate(totals, axis=0), placed]
        saved_scores.append(layer_scores)
    merged_stats = merged_2(tuple(stat_terms), "col", merge_stats)
    log_totals = []
    query_terms = []
    key_terms = []
    value_terms = []
    for layer_index in range(2):
        query_all = layers[layer_index][3]
        upstream_all = layers[layer_index][4]
        log_total = merged_stats[3 * layer_index] + jnp.log(merged_stats[3 * layer_index + 1])
        row_delta = merged_stats[3 * layer_index + 2]
        log_totals.append(log_total)
        query_parts = []
        key_parts = []
        value_parts = []
        for grouped_heads in range(SHARED_HEADS):
            head_low = grouped_heads * heads_per_group
            query_group = query_all[
                :, head_low * HEAD_SIZE : (head_low + heads_per_group) * HEAD_SIZE
            ].reshape(query_rows, heads_per_group, HEAD_SIZE)
            upstream_group = upstream_all[
                :, head_low * HEAD_SIZE : (head_low + heads_per_group) * HEAD_SIZE
            ].reshape(query_rows, heads_per_group, HEAD_SIZE)
            key_group = key_full[:, grouped_heads * HEAD_SIZE : (grouped_heads + 1) * HEAD_SIZE]
            value_group = value_full[:, grouped_heads * HEAD_SIZE : (grouped_heads + 1) * HEAD_SIZE]
            scores = saved_scores[layer_index][grouped_heads]
            weights = jnp.where(
                allowed[None],
                jnp.exp(scores - log_total[head_low : head_low + heads_per_group, :, None]),
                0.0,
            )
            slopes = jnp.einsum(
                "ihd,kd->hik", upstream_group, value_group, preferred_element_type=jnp.float32
            )
            dscore = (
                weights
                * (slopes - row_delta[head_low : head_low + heads_per_group, :, None])
                * score_scale
            ).astype(jnp.bfloat16)
            weights_low = weights.astype(jnp.bfloat16)
            value_parts.append(
                jnp.einsum(
                    "hik,ihd->kd", weights_low, upstream_group, preferred_element_type=jnp.float32
                )
            )
            key_parts.append(
                jnp.einsum("hik,ihd->kd", dscore, query_group, preferred_element_type=jnp.float32)
            )
            query_parts.append(
                jnp.einsum(
                    "hik,kd->ihd", dscore, key_group, preferred_element_type=jnp.float32
                ).reshape(query_rows, heads_per_group * HEAD_SIZE)
            )
        key_terms.append(jnp.concatenate(key_parts, axis=1))
        value_terms.append(jnp.concatenate(value_parts, axis=1))
        query_terms.append(jnp.concatenate(query_parts, axis=1))
    grad_one, grad_two = (
        lax.psum_scatter(query_terms[0], "col", scatter_dimension=1, tiled=True),
        lax.psum_scatter(query_terms[1], "col", scatter_dimension=1, tiled=True),
    )
    gradient_first = grad_one.astype(jnp.bfloat16)
    gradient_second = grad_two.astype(jnp.bfloat16)
    key_gradient_first, value_gradient_first, key_gradient_second, value_gradient_second = (
        lax.psum_scatter(key_terms[0], "row", scatter_dimension=1, tiled=True),
        lax.psum_scatter(value_terms[0], "row", scatter_dimension=1, tiled=True),
        lax.psum_scatter(key_terms[1], "row", scatter_dimension=1, tiled=True),
        lax.psum_scatter(value_terms[1], "row", scatter_dimension=1, tiled=True),
    )
    shared_key_gradient = (key_gradient_first + key_gradient_second).astype(jnp.bfloat16)
    shared_value_gradient = (value_gradient_first + value_gradient_second).astype(jnp.bfloat16)
    return (gradient_first, gradient_second, shared_key_gradient, shared_value_gradient)


def per_device(
    query_first,
    query_second,
    shared_key_states,
    shared_value_states,
    upstream_first,
    upstream_second,
    output_first,
    output_second,
    block_order,
):
    row_index = lax.axis_index("row")
    col_index = lax.axis_index("col")
    col_count = lax.axis_size("col")
    query_rows = query_first.shape[0]
    offsets = jnp.arange(BLK, dtype=jnp.int32)
    positions = (block_order[:, None] * BLK + offsets[None, :]).reshape(-1)
    key_rows = positions.shape[0] // col_count
    query_pos = lax.dynamic_slice_in_dim(positions, row_index * query_rows, query_rows)
    key_pos = lax.dynamic_slice_in_dim(positions, col_index * key_rows, key_rows)
    allowed = query_pos[:, None] >= key_pos[None, :]
    key_full, value_full = (
        lax.all_gather(shared_key_states, "row", axis=1, tiled=True),
        lax.all_gather(shared_value_states, "row", axis=1, tiled=True),
    )
    arrays = (
        query_first,
        query_second,
        upstream_first,
        upstream_second,
        output_first,
        output_second,
    )
    return grid_layout(arrays, key_full, value_full, allowed, col_index)


def solution(mesh):
    return jax.shard_map(
        per_device,
        mesh=mesh,
        in_specs=(
            P("row", "col"),
            P("row", "col"),
            P("col", "row"),
            P("col", "row"),
            P("row", "col"),
            P("row", "col"),
            P("row", "col"),
            P("row", "col"),
            P(),
        ),
        out_specs=(P("row", "col"), P("row", "col"), P("col", "row"), P("col", "row")),
        check_vma=False,
    )
```

profile of v0, /device:TPU:4, one launch (start us, length us, event | category | flops | bytes accessed | tf_op | source)
XLA Modules:
  0.0 716.7 jit_solution(9233990897268269214)
XLA Ops:
  11.0 17.4 %all_gather.56 = bf16[384,512]{0,1:T(8,128)(2,1)S(1)} all-gather(bf16[384,32]{0,1:T(8,128)(2,1)} %param.13), channel_id=1, replica_groups=mesh['row'=16,'col'=8] {'row'}, dimensions={1}, use_global_device_ids=true | all-gather | bytes 417792 | tf_op jit(solution)/shard_map/all_gather | solution.py:193
  30.1 36.2 %all_gather.71 = f32[8,64,192]{2,1,0:T(8,128)S(1)} all-gather(f32[1,64,192]{2,1,0:T(8,128)S(1)} %constant_dynamic-update-slice_fusion), channel_id=1, replica_groups=mesh['row'=16,'col'=8] {'col'}, dimensions={0}, use_global_device_ids=true | all-gather | bytes 442368 | tf_op jit(solution)/shard_map/all_gather | solution.py:18
  67.7 35.6 %all_gather.64 = f32[8,64,192]{2,1,0:T(8,128)S(1)} all-gather(f32[1,64,192]{2,1,0:T(8,128)S(1)} %constant_dynamic-update-slice_fusion.1), channel_id=1, replica_groups=mesh['row'=16,'col'=8] {'col'}, dimensions={0}, use_global_device_ids=true | all-gather | bytes 442368 | tf_op jit(solution)/shard_map/all_gather | solution.py:18
  104.1 18.4 %all_gather.72 = bf16[384,512]{0,1:T(8,128)(2,1)} all-gather(bf16[384,32]{0,1:T(8,128)(2,1)S(1)} %copy-done.48), channel_id=1, replica_groups=mesh['row'=16,'col'=8] {'row'}, dimensions={1}, use_global_device_ids=true | all-gather | bytes 417792 | tf_op jit(solution)/shard_map/all_gather | solution.py:194
  122.6 3.0 slice_bitcast_fusion.13
  128.6 18.9 %all-gather.11.cloned.1.call-done = bf16[192,8192]{1,0:T(8,128)(2,1)} async-done(((bf16[192,1024]{1,0:T(8,128)(2,1)}), bf16[192,8192]{1,0:T(8,128)(2,1)}) %all-gather.11.cloned.1.call-update) | async-done | bytes 3145744 | tf_op jit(solution)/shard_map/all_gather | solution.py:54
  155.4 3.0 fusion.131
  164.3 4.1 fusion.48
  168.4 14.9 %select_reduce_fusion.3 = (f32[16,192]{1,0:T(8,128)S(1)}, f32[16,192]{1,0:T(8,128)S(1)}, f32[16,192]{1,0:T(8,128)S(1)}, f32[16,192]{1,0:T(8,128)S(1)}, f32[16,19...) fusion(f32[384,192,16]{0,1,2:T(8,128)} %get-tuple-element.403, ...), kind=kOutput, calls=%fused_computation.81 | convolution fusion | flops 334995456 | bytes 38838272 | tf_op jit(solution)/shard_map/ihd,kd->hik/dot_general | solution.py:28
  183.3 11.9 %select_reduce_fusion.2 = (f32[16,192]{1,0:T(8,128)S(1)}, f32[16,192]{1,0:T(8,128)S(1)}, f32[16,192]{1,0:T(8,128)S(1)}, f32[16,192]{1,0:T(8,128)S(1)}, f32[16,192]{1,0:T(8,128)S(1)}, /*index=5*/f32[16,192]{1,0:T(8,128)S(1)}) fusion(f32[384,192,16]{0,1,2:T(8,128)} %fusion.131, f32[16,192]{1,0:T(8,128)S(1)} %get-tuple-element.328, ...), kind=kLoop, calls=%fused_computation.80 | loop fusion | flops 35371008 | bytes 28532736 | tf_op jit(solution)/shard_map/reduce_sum | solution.py:91
  195.2 35.7 %all-gather.3 = f32[512,192]{1,0:T(8,128)S(1)} all-gather(f32[64,192]{1,0:T(8,128)S(1)} %pad_maximum_fusion.5), channel_id=5, replica_groups=mesh['row'=16,'col'=8] {'col'}, dimensions={0}, use_global_device_ids=true | all-gather | bytes 442368 | tf_op jit(solution)/shard_map/all_gather | solution.py:18
  230.9 36.2 %all-gather.2 = f32[512,192]{1,0:T(8,128)S(1)} all-gather(f32[64,192]{1,0:T(8,128)S(1)} %pad_maximum_fusion.4), channel_id=4, replica_groups=mesh['row'=16,'col'=8] {'col'}, dimensions={0}, use_global_device_ids=true | all-gather | bytes 442368 | tf_op jit(solution)/shard_map/all_gather | solution.py:18
  267.1 35.8 %all-gather.1 = f32[512,192]{1,0:T(8,128)S(1)} all-gather(f32[64,192]{1,0:T(8,128)S(1)} %pad_maximum_fusion.3), channel_id=3, replica_groups=mesh['row'=16,'col'=8] {'col'}, dimensions={0}, use_global_device_ids=true | all-gather | bytes 442368 | tf_op jit(solution)/shard_map/all_gather | solution.py:18
  302.9 34.9 %all-gather = f32[512,192]{1,0:T(8,128)S(1)} all-gather(f32[64,192]{1,0:T(8,128)S(1)} %pad_maximum_fusion.2), channel_id=2, replica_groups=mesh['row'=16,'col'=8] {'col'}, dimensions={0}, use_global_device_ids=true | all-gather | bytes 442368 | tf_op jit(solution)/shard_map/all_gather | solution.py:18
  338.6 13.8 %while.25 = (s32[]{:T(128)}, f32[64,192]{1,0:T(8,128)S(1)}, f32[64,192]{1,0:T(8,128)S(1)}, f32[64,192]{1,0:T(8,128)S(1)}, f32[64,192]{1,0:T(8,128)S(1)}, /*index...) while((s32[]{:T(128)}, f32[64,192]{1,0:T(8,128)S(1)}, ...), condition=%wide.region_19.20_spmd, body=%wide.region_18.19_spmd.sunk | while | flops 172037 | bytes 884935 | solution.py:24
  352.5 3.3 slice_bitcast_fusion.7
  356.7 4.3 fusion.87
  364.0 5.0 fusion.96
  369.0 3.8 fusion.102
  382.5 4.1 fusion.15
  430.8 3.0 pad_maximum_fusion
  435.3 57.5 %reduce-scatter.9.cloned.1.call-done = f32[384,32]{0,1:T(8,128)} async-done(((f32[384,512]{0,1:T(8,128)}), f32[384,32]{0,1:T(8,128)}) %reduce-scatter.9.cloned.1.call-update) | async-done | bytes 49168 | tf_op jit(solution)/shard_map/reduce_scatter | solution.py:161
  494.2 111.3 %reduce-scatter.7.cloned.1.call-done = f32[192,1024]{1,0:T(8,128)} async-done(((f32[192,8192]{1,0:T(8,128)}), f32[192,1024]{1,0:T(8,128)}) %reduce-scatter.7.cloned.1.call-update) | async-done | bytes 786448 | tf_op jit(solution)/shard_map/reduce_scatter | solution.py:156
  607.5 100.2 %reduce-scatter.5.cloned.1.call-done = f32[192,1024]{1,0:T(8,128)} async-done(((f32[192,8192]{1,0:T(8,128)}), f32[192,1024]{1,0:T(8,128)}) %reduce-scatter.5.cloned.1.call-update) | async-done | bytes 786448 | tf_op jit(solution)/shard_map/reduce_scatter | solution.py:155
  (294 shorter events, 102.3 us)
Async XLA Ops:
  7.2 59.9 %copy-start.28 = (bf16[192,1024]{1,0:T(8,128)(2,1)S(1)}, bf16[192,1024]{1,0:T(8,128)(2,1)}, u32[]{:S(2)}) copy-start(bf16[192,1024]{1,0:T(8,128)(2,1)} %param.15) | copy-start | bytes 1179652
  7.2 59.9 %copy-start.46 = (bf16[192,1024]{1,0:T(8,128)(2,1)S(1)}, bf16[192,1024]{1,0:T(8,128)(2,1)}, u32[]{:S(2)}) copy-start(bf16[192,1024]{1,0:T(8,128)(2,1)} %param.17) | copy-start | bytes 1179652
  7.2 115.5 %all-gather.9.cloned.1.call-start = ((), (), s32[]{:S(2)}) async-start(), calls=%async_computation.4 | async-start | bytes 3538944 | tf_op jit(solution)/shard_map/all_gather | solution.py:53
  7.9 139.6 %all-gather.11.cloned.1.call-start = ((), (), s32[]{:S(2)}) async-start(), calls=%async_computation.5 | async-start | bytes 3538944 | tf_op jit(solution)/shard_map/all_gather | solution.py:54
  8.7 343.8 %all-gather.13.cloned.1.call-start = ((), (), s32[]{:S(2)}) async-start(), calls=%async_computation.6 | async-start | bytes 3538944 | tf_op jit(solution)/shard_map/all_gather | solution.py:55
  9.4 351.6 %all-gather.15.cloned.1.call-start = ((), (), s32[]{:S(2)}) async-start(), calls=%async_computation.8 | async-start | bytes 3538944 | tf_op jit(solution)/shard_map/all_gather | solution.py:56
  10.0 423.9 %reduce-scatter.11.cloned.1.call-start = ((), (), s32[]{:S(2)}) async-start(), calls=%async_computation.11 | async-start | bytes 835584 | tf_op jit(solution)/shard_map/reduce_scatter | solution.py:162
  28.3 75.8 %copy-start.48 = (bf16[384,32]{0,1:T(8,128)(2,1)S(1)}, bf16[384,32]{0,1:T(8,128)(2,1)}, u32[]{:S(2)}) copy-start(bf16[384,32]{0,1:T(8,128)(2,1)} %param.14) | copy-start | bytes 73732
  155.4 8.9 %slice-start = ((s8[4718592]{0:T(1024)(128)(4,1)}), s8[4194304]{0:T(1024)(128)(4,1)S(1)}, s32[]{:S(2)}) async-start(s8[4718592]{0:T(1024)(128)(4,1)} %bitcast.540), calls=%async_computation.12 | async-start | bytes 8388608
  230.9 106.9 %copy-start.24 = (f32[512,192]{1,0:T(8,128)}, f32[512,192]{1,0:T(8,128)S(1)}, u32[]{:S(2)}) copy-start(f32[512,192]{1,0:T(8,128)S(1)} %all-gather.3) | copy-start | bytes 1179652
  267.1 70.7 %copy-start.25 = (f32[512,192]{1,0:T(8,128)}, f32[512,192]{1,0:T(8,128)S(1)}, u32[]{:S(2)}) copy-start(f32[512,192]{1,0:T(8,128)S(1)} %all-gather.2) | copy-start | bytes 1179652
  302.9 34.9 %copy-start.26 = (f32[512,192]{1,0:T(8,128)}, f32[512,192]{1,0:T(8,128)S(1)}, u32[]{:S(2)}) copy-start(f32[512,192]{1,0:T(8,128)S(1)} %all-gather.1) | copy-start | bytes 1179652
  352.4 10.8 %copy-start.55 = (f32[16,192]{1,0:T(8,128)}, f32[16,192]{1,0:T(8,128)S(1)}, u32[]{:S(2)}) copy-start(f32[16,192]{1,0:T(8,128)S(1)} %get-tuple-element.387) | copy-start | bytes 36868
  352.4 16.6 %copy-start.51 = (f32[16,192]{1,0:T(8,128)}, f32[16,192]{1,0:T(8,128)S(1)}, u32[]{:S(2)}) copy-start(f32[16,192]{1,0:T(8,128)S(1)} %get-tuple-element.389) | copy-start | bytes 36868
  352.4 20.5 %copy-start.49 = (f32[16,192]{1,0:T(8,128)}, f32[16,192]{1,0:T(8,128)S(1)}, u32[]{:S(2)}) copy-start(f32[16,192]{1,0:T(8,128)S(1)} %get-tuple-element.388) | copy-start | bytes 36868
  352.5 27.3 %copy-start.53 = (f32[16,192]{1,0:T(8,128)}, f32[16,192]{1,0:T(8,128)S(1)}, u32[]{:S(2)}) copy-start(f32[16,192]{1,0:T(8,128)S(1)} %get-tuple-element.390) | copy-start | bytes 36868
  363.1 9.7 %copy-start.40 = (bf16[24,16,8,128]{3,2,1,0:T(8,128)(2,1)}, bf16[24,16,8,128]{3,2,1,0:T(8,128)(2,1)S(1)}, u32[]{:S(2)}) copy-start(bf16[24,16,8,128]{3,2,1,0:T(8,128)(2,1)S(1)} %get-tuple-element.373) | copy-start | bytes 2359300
  363.1 9.8 %copy-start.38 = (bf16[24,16,8,128]{3,2,1,0:T(8,128)(2,1)}, bf16[24,16,8,128]{3,2,1,0:T(8,128)(2,1)S(1)}, u32[]{:S(2)}) copy-start(bf16[24,16,8,128]{3,2,1,0:T(8,128)(2,1)S(1)} %get-tuple-element.372) | copy-start | bytes 2359300
  363.2 16.6 %copy-start.42 = (bf16[24,16,8,128]{3,2,1,0:T(8,128)(2,1)}, bf16[24,16,8,128]{3,2,1,0:T(8,128)(2,1)S(1)}, u32[]{:S(2)}) copy-start(bf16[24,16,8,128]{3,2,1,0:T(8,128)(2,1)S(1)} %get-tuple-element.374) | copy-start | bytes 2359300
  363.2 9.7 %slice-start.14 = ((s8[4718592]{0:T(1024)(128)(4,1)}), s8[4194304]{0:T(1024)(128)(4,1)S(1)}, s32[]{:S(2)}) async-start(s8[4718592]{0:T(1024)(128)(4,1)} %bitcast.554), calls=%async_computation.26 | async-start | bytes 8388608
  381.2 6.7 slice-start.22
  382.2 110.6 %reduce-scatter.9.cloned.1.call-start = ((), (), s32[]{:S(2)}) async-start(), calls=%async_computation.10 | async-start | bytes 835584 | tf_op jit(solution)/shard_map/reduce_scatter | solution.py:161
  415.4 190.2 %reduce-scatter.7.cloned.1.call-start = ((), (), s32[]{:S(2)}) async-start(), calls=%async_computation.9 | async-start | bytes 7077888 | tf_op jit(solution)/shard_map/reduce_scatter | solution.py:156
  424.1 283.6 %reduce-scatter.5.cloned.1.call-start = ((), (), s32[]{:S(2)}) async-start(), calls=%async_computation.7 | async-start | bytes 7077888 | tf_op jit(solution)/shard_map/reduce_scatter | solution.py:155
  (66 other events, 200.5 us)
Sparse Core Ops, SparseCore 0:
  10.4 71.7 all-gather.8
  84.5 62.9 all-gather.10
  149.9 63.6 all-gather.12
  215.8 69.6 all-gather.14
  382.3 48.3 reduce-scatter.10
  433.0 59.7 reduce-scatter.8
  496.7 108.7 reduce-scatter.6
  610.0 97.6 reduce-scatter.4
where the time goes:
time: 728 us; the launch traced here: 717 us
  waiting for transfers between devices  291 us (40%)
  blocking collectives  250 us (34%)
  matrix products  91 us (12%)
  other arithmetic  42.9 us (6%)
  local copies, waits for them, and re-layouts  25.5 us (4%)
  between operations  15.8 us (2%)
    all_gather x6, blocking collectives, merged_2(): everything = jax.tree.map(lambda part: lax.all_gather(part, axis), value)  214 us
    reduce_scatter x1, waiting for transfers between devices, grid_layout(): lax.psum_scatter(query_terms[1], 'col', scatter_dimension=1, tiled=True)  111 us
    reduce_scatter x1, waiting for transfers between devices, grid_layout(): lax.psum_scatter(query_terms[0], 'col', scatter_dimension=1, tiled=True)  100 us
    reduce_scatter x1, waiting for transfers between devices, grid_layout(): lax.psum_scatter(key_terms[0], 'row', scatter_dimension=1, tiled=True)  57.5 us
    dot_general x8, matrix products, head_scores(): jnp.einsum('ihd,kd->hik', query_group, key_group, preferred_element_type=...  36.5 us
    unnamed x170, local copies, waits for them, and re-layouts  23.7 us
    dot_general x8, matrix products, grid_layout(): jnp.einsum('hik,ihd->kd', weights_low, upstream_group, preferred_element_...  20.2 us
    dot_general x8, matrix products, grid_layout(): jnp.einsum('ihd,kd->hik', upstream_group, value_group, preferred_element_...  19.5 us
  transfers between devices with their start and end apart: 8, of which 4 were waited for; matrix products, arithmetic and copies ran while one was open for 18% of the time, Pallas kernels for 0%

commit v1 on v0

v1 whole, which is shorter than its diff:
```python
import math

import jax
import jax.numpy as jnp
from jax import lax
from jax.experimental import pallas as pl
from jax.experimental.pallas import tpu as pltpu
from jax.sharding import Mesh
from jax.sharding import PartitionSpec as P

HEAD = 128
BLK = 64
CHUNK = 256
LADDER = (8, 4, 2, 1)
SCALE = 1.0 / math.sqrt(HEAD)
SCALE_LOG2 = SCALE * math.log2(math.e)
NEG = -1e30
SAFE = 2.0**60
F32 = jnp.float32
BF16 = jnp.bfloat16
AXES = ("x", "zl", "core", "y", "zh")


def nt(a, b):
    return lax.dot_general(a, b, (((1,), (1,)), ((), ())), preferred_element_type=F32)


def nn(a, b):
    return jnp.dot(a, b, preferred_element_type=F32)


def fold_rows(value, combine):
    return combine(value.reshape(value.shape[0] // 8, 8, value.shape[1]), axis=0)


def stacked(value):
    heads = value.shape[1] // HEAD
    return jnp.concatenate([value[:, h * HEAD : (h + 1) * HEAD] for h in range(heads)], axis=0)


def attention_kernel(order_ref, place_ref, *refs):
    piece_refs, own_refs, other_ref, refs = refs[:8], refs[8:14], refs[14], refs[15:]
    dq_own_ref, dq_other_ref, keep_ref, give_ref = refs[:4]
    wide_ref, k_ref, kt_ref, v_ref, s_ref, dk_ref, dv_ref, dqt_ref = refs[4:12]
    qs_ref, us_ref, peak_ref, total_ref, pieces_ref, rows_ref, sems = refs[12:]
    step = pl.program_id(0)
    steps = pl.num_programs(0)
    keys = k_ref.shape[0]
    blocks = keys // BLK
    lanes = s_ref.shape[1]
    core, x, z = [place_ref[i] for i in range(3)]

    def tile(start, t):
        return pl.ds(pl.multiple_of(start * t, t), t)

    def piece_copy(i):
        return pltpu.make_async_copy(piece_refs[i], pieces_ref.at[i], sems.at[i])

    def own_copy(i, layer=0):
        return pltpu.make_async_copy(own_refs[2 * i + layer], rows_ref.at[i], sems.at[8 + i])

    def other_copy():
        return pltpu.make_async_copy(other_ref, rows_ref.at[pl.ds(3, 3)], sems.at[11])

    @pl.when(step == 0)
    def _():
        for i in range(8):
            piece_copy(i).start()
        for layer in range(2):

            @pl.when(core == layer)
            def _(layer=layer):
                for i in range(3):
                    own_copy(i, layer).start()

        other_copy().start()
        for i in range(8):
            piece_copy(i).wait()
        for which in range(2):
            for side in range(2):
                core_at = core if side == 0 else 1 - core
                for dz in range(4):
                    z_at = (z + 4 - dz) % 4
                    sub = (z_at % 2) * 2 + core_at
                    for dx in range(4):
                        col = ((x + 4 - dx) % 4) * 2 + z_at // 2
                        wide_ref[tile(sub, 32), tile(col, 384)] = pieces_ref[
                            side * 4 + dz, dx, which
                        ].astype(F32)
            for t in range(keys // 128):
                part = wide_ref[:, t * 128 : (t + 1) * 128].T.astype(BF16)
                for half in range(2):
                    rows = part[half * BLK : half * BLK + BLK]
                    if which == 0:
                        k_ref[tile(order_ref[2 * t + half], BLK), :] = rows
                    else:
                        v_ref[tile(order_ref[2 * t + half], BLK), :HEAD] = rows
        for t in range(keys // 128):
            kt_ref[:, t * 128 : (t + 1) * 128] = (
                k_ref[t * 128 : (t + 1) * 128, :].astype(F32).T.astype(BF16)
            )
        lane = lax.broadcasted_iota(jnp.int32, (keys, HEAD), 1)
        v_ref[:, HEAD:] = jnp.where(lane < 3, -1.0, 0.0).astype(BF16)
        dk_ref[...] = jnp.zeros_like(dk_ref)
        dv_ref[...] = jnp.zeros_like(dv_ref)

    side = step // (steps // 2)

    @pl.when(step == 0)
    def _():
        for i in range(3):
            own_copy(i).wait()

    @pl.when(step == steps // 2)
    def _():
        other_copy().wait()

    block = tile(step % (steps // 2), BLK)
    query, upstream, output = [stacked(rows_ref[side * 3 + j, block, :]) for j in range(3)]
    delta = jnp.sum(upstream.astype(F32) * output.astype(F32), axis=1, keepdims=True)
    high = delta.astype(BF16).astype(F32)
    rest = delta - high
    middle = rest.astype(BF16).astype(F32)
    lane = lax.broadcasted_iota(jnp.int32, query.shape, 1)
    tail = jnp.where(
        lane == 0, high, jnp.where(lane == 1, middle, jnp.where(lane == 2, rest - middle, 0.0))
    )
    qs_ref[...] = query
    us_ref[:, :HEAD] = upstream
    us_ref[:, HEAD:] = tail.astype(BF16)

    row = (x * 2 + z % 2) * 2 + jnp.where(side == 0, core, 1 - core)
    own = order_ref[row * (steps // 2) + step % (steps // 2)]
    last = own // (CHUNK // BLK)

    def rows(base, size):
        return pl.ds(pl.multiple_of(base * CHUNK, CHUNK), size * CHUNK)

    def ladder(count, body):
        done = 0
        for size in LADDER:
            laps = (count - done) // size
            lax.fori_loop(
                0, laps, lambda j, c, done=done, size=size: (body(done + j * size, size), c)[1], 0
            )
            done = done + laps * size

    def edge():
        key_at = last * CHUNK + lax.broadcasted_iota(jnp.int32, (CHUNK, lanes), 0)
        query_at = own * BLK + lax.broadcasted_iota(jnp.int32, (CHUNK, lanes), 1) % BLK
        return jnp.where(query_at >= key_at, nt(k_ref[rows(last, 1), :], qs_ref[...]), NEG)

    def expo(scores, where):
        part = jnp.exp2((scores - peak_ref[...]) * SCALE_LOG2)
        s_ref[where, :] = part
        total_ref[...] += fold_rows(part, jnp.sum)

    def column_max(scores):
        return jnp.max(fold_rows(scores, jnp.max), axis=0, keepdims=True)

    def forward(scores):
        total_ref[...] = jnp.zeros_like(total_ref)
        expo(scores, rows(last, 1))
        ladder(
            last,
            lambda base, size: expo(nt(k_ref[rows(base, size), :], qs_ref[...]), rows(base, size)),
        )

    scores = edge()
    peak_ref[...] = column_max(scores)
    forward(scores)

    @pl.when(jnp.logical_not(jnp.max(total_ref[...]) < SAFE))
    def _():
        def widen(j, carry):
            scores = nt(k_ref[rows(j, 1), :], qs_ref[...])
            peak_ref[...] = jnp.maximum(peak_ref[...], column_max(scores))
            return carry

        lax.fori_loop(0, last, widen, 0)
        forward(edge())

    inverse = 1.0 / jnp.sum(total_ref[...], axis=0, keepdims=True)
    dqt_ref[...] = jnp.zeros_like(dqt_ref)

    def grads(base, size):
        at = rows(base, size)
        probs = s_ref[at, :] * inverse
        dscore = (probs * nt(v_ref[at, :], us_ref[...])).astype(BF16)
        dv_ref[at, :] += nn(probs.astype(BF16), us_ref[:, :HEAD])
        dk_ref[at, :] += nn(dscore, qs_ref[...])
        dqt_ref[...] += nn(kt_ref[:, at], dscore)

    ladder(last + 1, grads)

    dq = (dqt_ref[...] * SCALE).T.astype(BF16)
    for i, ref in enumerate((dq_own_ref, dq_other_ref)):

        @pl.when(side == i)
        def _(ref=ref):
            for h in range(lanes // BLK):
                ref[:, h * HEAD : (h + 1) * HEAD] = dq[h * BLK : (h + 1) * BLK]

    @pl.when(step == steps - 1)
    def _():
        for which in range(2):
            source = dk_ref if which == 0 else dv_ref
            for t in range(keys // 128):
                part = jnp.concatenate(
                    [source[tile(order_ref[2 * t + half], BLK), :] for half in range(2)], axis=0
                )
                if which == 0:
                    part = part * SCALE
                wide_ref[:, t * 128 : (t + 1) * 128] = part.T
            for b in range(4):
                for z_to in range(4):
                    slot = (b * 2 + z_to % 2) * 2 + z_to // 2
                    col = b * 2 + z_to // 2
                    for ref, core_to in ((keep_ref, core), (give_ref, 1 - core)):
                        sub = (z_to % 2) * 2 + core_to
                        ref[slot, which] = wide_ref[
                            tile(sub, 32), col * 384 : col * 384 + 384
                        ].astype(ref.dtype)


def attention(order, place, pieces, arrays):
    half = arrays[0].shape[0] // BLK
    heads = arrays[0].shape[1] // HEAD
    lanes = heads * BLK
    piece = pieces[0].shape
    keys = 8 * piece[-1]
    whole = lambda shape: pl.BlockSpec(shape, lambda i, *s: (0,) * len(shape))
    first = lambda i: jnp.minimum(i, half - 1)
    second = lambda i: jnp.maximum(i - half, 0)
    rows = (BLK, heads * HEAD)
    gradient = jax.ShapeDtypeStruct((half * BLK, heads * HEAD), BF16)
    parts = (16,) + piece[1:]
    return pl.pallas_call(
        attention_kernel,
        grid_spec=pltpu.PrefetchScalarGridSpec(
            num_scalar_prefetch=2,
            grid=(2 * half,),
            in_specs=[pl.BlockSpec(memory_space=pl.ANY)] * 15,
            out_specs=[
                pl.BlockSpec(rows, lambda i, *s: (first(i), 0)),
                pl.BlockSpec(rows, lambda i, *s: (second(i), 0)),
                whole(parts),
                whole(parts),
            ],
            scratch_shapes=[
                pltpu.VMEM((HEAD, keys), F32),
                pltpu.VMEM((keys, HEAD), BF16),
                pltpu.VMEM((HEAD, keys), BF16),
                pltpu.VMEM((keys, 2 * HEAD), BF16),
                pltpu.VMEM((keys, lanes), F32),
                pltpu.VMEM((keys, HEAD), F32),
                pltpu.VMEM((keys, HEAD), F32),
                pltpu.VMEM((HEAD, lanes), F32),
                pltpu.VMEM((lanes, HEAD), BF16),
                pltpu.VMEM((lanes, 2 * HEAD), BF16),
                pltpu.VMEM((1, lanes), F32),
                pltpu.VMEM((8, lanes), F32),
                pltpu.VMEM((8,) + piece, BF16),
                pltpu.VMEM((6,) + arrays[0].shape, BF16),
                pltpu.SemaphoreType.DMA((12,)),
            ],
        ),
        out_shape=[
            gradient,
            gradient,
            jax.ShapeDtypeStruct(parts, BF16),
            jax.ShapeDtypeStruct(parts, BF16),
        ],
        compiler_params=pltpu.CompilerParams(vmem_limit_bytes=56 * 1024 * 1024),
        name="attention",
    )(order, place, *pieces, *arrays)


def moved(value, target):
    def index(x, z, core, y):
        return (((x * 2 + z % 2) * 2 + core) * 4 + y) * 2 + z // 2

    pairs = [
        (index(x, z, core, y), index(*target(x, z, core, y)))
        for x in range(4)
        for z in range(4)
        for core in range(2)
        for y in range(4)
    ]
    return lax.ppermute(value, AXES, pairs)


def swap_cores(value):
    return lax.ppermute(value, "core", [(0, 1), (1, 0)])


def spread(piece):
    parts = jnp.stack(
        [moved(piece, lambda x, z, core, y, d=d: ((y + d) % 4, z, core, x)) for d in range(4)]
    )
    return [parts] + [
        moved(parts, lambda x, z, core, y, d=d: (x, (z + d) % 4, core, y)) for d in (1, 2, 3)
    ]


def reduce_pieces(keep, give):
    chip = (keep.astype(F32) + swap_cores(give).astype(F32)).astype(BF16)
    parts = lax.all_to_all(chip, ("x", "zl", "zh"), 0, 0)
    total = jnp.sum(parts.astype(F32), axis=0).astype(BF16)
    return moved(total, lambda x, z, core, y: (y, z, core, x))


def per_device(q1, q2, keys, values, u1, u2, o1, o2, block_order):
    x, core = lax.axis_index("x"), lax.axis_index("core")
    z = lax.axis_index("zh") * 2 + lax.axis_index("zl")
    place = jnp.stack([core, x, z]).astype(jnp.int32)
    own = (q1, q2, u1, u2, o1, o2)
    other = swap_cores(jnp.where(core == 0, jnp.stack(own[1::2]), jnp.stack(own[::2])))
    pieces = spread(jnp.stack([keys.T, values.T]))
    pieces = pieces + [swap_cores(piece) for piece in pieces]
    dq_own, dq_other, keep, give = attention(block_order, place, pieces, (*own, other))
    dq_back = swap_cores(dq_other)
    sums = reduce_pieces(keep, give)
    dq1 = jnp.where(core == 0, dq_own, dq_back)
    dq2 = jnp.where(core == 0, dq_back, dq_own)
    return dq1, dq2, sums[0].T, sums[1].T


def solution(mesh):
    split = Mesh(mesh.devices.reshape(4, 2, 2, 4, 2), AXES)
    row, col = ("x", "zl", "core"), ("y", "zh")
    wide, narrow = P(row, col), P(col, row)
    return jax.shard_map(
        per_device,
        mesh=split,
        in_specs=(wide, wide, narrow, narrow, wide, wide, wide, wide, P()),
        out_specs=(wide, wide, narrow, narrow),
        check_vma=False,
    )
```

time: 728 us -> 101 us (0.14); the launches traced: 717 us -> 100 us
  waiting for transfers between devices: 291 us -> 33.2 us
  blocking collectives: 250 us -> 0 us
  matrix products: 91 us -> 0 us
  other arithmetic: 42.9 us -> 5.77 us
  Pallas kernels: 0 us -> 31.4 us
  starting transfers between devices: 0.7 us -> 27.1 us
  local copies, waits for them, and re-layouts: 25.5 us -> 1.7 us
  between operations: 15.8 us -> 0.86 us
    reduce_scatter x4 -> x0, waiting for transfers between devices: 269 us -> none  [the longest x1 111 us: grid_layout(): lax.psum_scatter(query_terms[1], 'col', scatter_dimension=1, tiled=True)]
    all_gather x8 -> x0, blocking collectives: 250 us -> none  [the longest x6 214 us: merged_2(): everything = jax.tree.map(lambda part: lax.all_gather(part, axis), value)]
    dot_general x40 -> x0, matrix products: 91 us -> none  [the longest x8 36.5 us: head_scores(): jnp.einsum('ihd,kd->hik', query_group, key_group, preferred_element_type=...]
    pallas_call x0 -> x1, Pallas kernels: none -> 31.4 us  [attention(): pl.pallas_call(attention_kernel, grid_spec=pltpu.PrefetchScalarGridSpec(n...]
    unnamed x170 -> x22, local copies, waits for them, and re-layouts: 23.7 us -> 1.08 us
    ppermute x0 -> x15, starting transfers between devices: none -> 22.1 us  [the longest x8 21.6 us: moved(): return lax.ppermute(value, AXES, pairs)]
    ppermute x0 -> x15, waiting for transfers between devices: none -> 19.8 us  [the longest x8 16.7 us: moved(): return lax.ppermute(value, AXES, pairs)]
    all_gather x4 -> x0, waiting for transfers between devices: 19 us -> none  [the longest x1 18.9 us: grid_layout(): lax.all_gather(query_second, 'col', axis=1, tiled=True)]
  transfers between devices with their start and end apart: 8 -> 16, of which waited for: 4 -> 8; matrix products, arithmetic and copies ran while one was open for 18% -> 2% of each run, Pallas kernels for 0% -> 0%
where the time goes in v1:
time: 101 us; the launch traced here: 100 us
  waiting for transfers between devices  33.2 us (33%)
  Pallas kernels  31.4 us (31%)
  starting transfers between devices  27.1 us (27%)
  other arithmetic  5.77 us (6%)
  local copies, waits for them, and re-layouts  1.7 us (2%)
    pallas_call x1, Pallas kernels, attention(): pl.pallas_call(attention_kernel, grid_spec=pltpu.PrefetchScalarGridSpec(n...  31.4 us
    ppermute x8, starting transfers between devices, moved(): return lax.ppermute(value, AXES, pairs)  21.6 us
    ppermute x8, waiting for transfers between devices, moved(): return lax.ppermute(value, AXES, pairs)  16.7 us
    all_to_all x1, waiting for transfers between devices, reduce_pieces(): parts = lax.all_to_all(chip, ('x', 'zl', 'zh'), 0, 0)  13.3 us
    all_to_all x1, starting transfers between devices, reduce_pieces(): parts = lax.all_to_all(chip, ('x', 'zl', 'zh'), 0, 0)  4.96 us
    ppermute x7, waiting for transfers between devices, swap_cores(): return lax.ppermute(value, 'core', [(0, 1), (1, 0)])  3.19 us
    convert_element_type x1, other arithmetic, reduce_pieces(): chip = (keep.astype(F32) + swap_cores(give).astype(F32)).astype(BF16)  2.26 us
  transfers between devices with their start and end apart: 16, of which 8 were waited for; matrix products, arithmetic and copies ran while one was open for 2% of the time, Pallas kernels for 0%

profile of v1, /device:TPU:4, one launch (start us, length us, event | category | flops | bytes accessed | tf_op | source)
XLA Modules:
  0.0 100.0 jit_solution(7239409623899037130)
XLA Ops:
  0.7 1.8 %maximum_select_fusion = bf16[3,192,1024]{2,1,0:T(8,128)(2,1)S(1)} fusion(bf16[1,192,1024]{2,1,0:T(8,128)(2,1)} %bitcast.32, bf16[1,192,1024]{2,1,0:T(8,128)(2,1)} %bitcast.30, bf16[1,192,1024]{2,1,0:T(8,128)(2,1)} %bitcast.28, bf16[1,192,1024]{2,1,0:T(8,128)(2,1)} %bitcast.31, bf16[1,192,1024]{2,1,0:T(8,128)(2,1)} %bitcast.29, ...), kind=kLoop, calls=%fused_computation.1 | loop fusion | flops 2949120 | bytes 3538945 | tf_op jit(solution)/shard_map/jit(_where)/select_n | solution.py:318
  2.6 3.9 %collective-permute-start.3 = (bf16[2,32,384]{2,1,0:T(8,128)(2,1)S(1)}, bf16[2,32,384]{2,1,0:T(8,128)(2,1)S(1)}, u32[]{:S(2)}, u32[]{:S(2)}) collective-permute-start(bf16[2,32,384]{2,1,0:T(8,128)(2,1)S(1)} %pad_maximum_fusion.1), channel_id=1, source_target_pairs={{0,96},{2,0},{4,32},{6,64},{8,104},{10,8},{12,40},{14,72},{16,112}... | collective-permute-start | bytes 147464 | tf_op jit(solution)/shard_map/ppermute | solution.py:290
  6.5 0.1 collective-permute-start.1
  6.6 7.6 %collective-permute-start = (bf16[2,32,384]{2,1,0:T(8,128)(2,1)S(1)}, bf16[2,32,384]{2,1,0:T(8,128)(2,1)S(1)}, u32[]{:S(2)}, u32[]{:S(2)}) collective-permute-start(bf16[2,32,384]{2,1,0:T(8,128)(2,1)S(1)} %pad_maximum_fusion.1), channel_id=1, source_target_pairs={{0,0},{2,32},{4,64},{6,96},{8,8},{10,40},{12,72},{14,104},{16,16},... | collective-permute-start | bytes 147464 | tf_op jit(solution)/shard_map/ppermute | solution.py:290
  14.3 2.5 %collective-permute-done = bf16[2,32,384]{2,1,0:T(8,128)(2,1)S(1)} collective-permute-done((bf16[2,32,384]{2,1,0:T(8,128)(2,1)S(1)}, bf16[2,32,384]{2,1,0:T(8,128)(2,1)S(1)}, u32[]{:S(2)}, u32[]{:S(2)}) %collective-permute-start) | collective-permute-done | bytes 49184 | tf_op jit(solution)/shard_map/ppermute | solution.py:290
  16.8 4.1 %collective-permute-start.6 = (bf16[4,2,32,384]{3,2,1,0:T(8,128)(2,1)S(1)}, bf16[4,2,32,384]{3,2,1,0:T(8,128)(2,1)S(1)}, u32[]{:S(2)}, u32[]{:S(2)}) collective-permute-start(bf16[4,2,32,384]{3,2,1,0:T(8,128)(2,1)S(1)} %pad_maximum_fusion.refs_0_), channel_id=1, source_target_pairs={{0,17},{2,19},{4,21},{6,23},{8,25},{10,27},{12,29},{14,31},{16,0},... | collective-permute-start | bytes 589832 | tf_op jit(solution)/shard_map/ppermute | solution.py:290
  20.9 1.3 %collective-permute-start.4 = (bf16[4,2,32,384]{3,2,1,0:T(8,128)(2,1)S(1)}, bf16[4,2,32,384]{3,2,1,0:T(8,128)(2,1)S(1)}, u32[]{:S(2)}, u32[]{:S(2)}) collective-permute-start(bf16[4,2,32,384]{3,2,1,0:T(8,128)(2,1)S(1)} %pad_maximum_fusion.refs_0_), channel_id=1, source_target_pairs={{0,16},{2,18},{4,20},{6,22},{8,24},{10,26},{12,28},{14,30},{16,1},... | collective-permute-start | bytes 589832 | tf_op jit(solution)/shard_map/ppermute | solution.py:290
  22.2 6.5 %collective-permute-done.6.refs_3_ = bf16[4,2,32,384]{3,2,1,0:T(8,128)(2,1)S(1)} collective-permute-done((bf16[4,2,32,384]{3,2,1,0:T(8,128)(2,1)S(1)}, bf16[4,2,32,384]{3,2,1,0:T(8,128)(2,1)S(1)}, u32[]{:S(2)}, u32[]{:S(2)}) %collective-permute-start.6) | collective-permute-done | bytes 196640 | tf_op jit(solution)/shard_map/ppermute | solution.py:290
  28.7 1.6 %collective-permute-done.5.refs_2_ = bf16[4,2,32,384]{3,2,1,0:T(8,128)(2,1)S(1)} collective-permute-done((bf16[4,2,32,384]{3,2,1,0:T(8,128)(2,1)S(1)}, bf16[4,2,32,384]{3,2,1,0:T(8,128)(2,1)S(1)}, u32[]{:S(2)}, u32[]{:S(2)}) %collective-permute-start.5) | collective-permute-done | bytes 196640 | tf_op jit(solution)/shard_map/ppermute | solution.py:290
  30.3 1.8 %collective-permute-done.4.refs_1_ = bf16[4,2,32,384]{3,2,1,0:T(8,128)(2,1)S(1)} collective-permute-done((bf16[4,2,32,384]{3,2,1,0:T(8,128)(2,1)S(1)}, bf16[4,2,32,384]{3,2,1,0:T(8,128)(2,1)S(1)}, u32[]{:S(2)}, u32[]{:S(2)}) %collective-permute-start.4) | collective-permute-done | bytes 196640 | tf_op jit(solution)/shard_map/ppermute | solution.py:290
  32.1 0.6 pad_add_fusion.place_ref
  32.7 0.9 collective-permute-done.8.refs_5_
  33.7 1.0 %copy-done = bf16[3,192,1024]{2,1,0:T(8,128)(2,1)} copy-done((bf16[3,192,1024]{2,1,0:T(8,128)(2,1)}, bf16[3,192,1024]{2,1,0:T(8,128)(2,1)S(1)}, u32[]{:S(2)}) %copy-start) | copy-done | bytes 1179672
  34.7 31.4 %attention.1 = (bf16[192,1024]{1,0:T(8,128)(2,1)}, bf16[192,1024]{1,0:T(8,128)(2,1)}, bf16[16,2,32,384]{3,2,1,0:T(8,128)(2,1)}, bf16[16,2,32,384]{3,2,1,0:T(8,128)(2,1)}) custom-call(s32[48]{0:T(128)} %order_ref.1, s32[3]{0:T(128)} %pad_add_fusion.place_ref, bf16[4,2,32,384]{3,2,1,0:T(8,128)(2,1)} %copy-done.1, bf16[4,2,32,384]{3,2,1,0:T(8,128)(2,1)} %copy-done.5, ...), custom_call_target="tpu_custom_call" | custom-call | tf_op jit(solution)/shard_map/attention/pallas_call | solution.py:238
  66.2 0.3 collective-permute-start.13
  66.5 2.2 %collective-permute-done.13 = bf16[16,2,32,384]{3,2,1,0:T(8,128)(2,1)S(1)} collective-permute-done((bf16[16,2,32,384]{3,2,1,0:T(8,128)(2,1)}, bf16[16,2,32,384]{3,2,1,0:T(8,128)(2,1)S(1)}, u32[]{:S(2)}, u32[]{:S(2)}) %collective-permute-start.13) | collective-permute-done | bytes 786464 | tf_op jit(solution)/shard_map/ppermute | solution.py:294
  68.8 2.3 %add_convert_fusion = bf16[16,2,32,384]{3,2,1,0:T(8,128)(2,1)} fusion(bf16[16,2,32,384]{3,2,1,0:T(8,128)(2,1)S(1)} %collective-permute-done.13, bf16[16,2,32,384]{3,2,1,0:T(8,128)(2,1)} %get-tuple-element.10), kind=kLoop, calls=%fused_computation | loop fusion | flops 1572864 | bytes 2359296 | tf_op jit(solution)/shard_map/convert_element_type | solution.py:307
  71.0 5.0 %all-to-all-start = ((bf16[16,2,32,384]{3,2,1,0:T(8,128)(2,1)}), bf16[16,2,32,384]{3,2,1,0:T(8,128)(2,1)S(1)}, u32[]{:S(2)}, u32[]{:S(2)}) async-start(bf16[16,2,32,384]{3,2,1,0:T(8,128)(2,1)} %add_convert_fusion), calls=%async_computation | async-start | bytes 1572864 | tf_op jit(solution)/shard_map/all_to_all | solution.py:308
  76.1 13.3 %all-to-all-done = bf16[16,2,32,384]{3,2,1,0:T(8,128)(2,1)S(1)} async-done(((bf16[16,2,32,384]{3,2,1,0:T(8,128)(2,1)}), bf16[16,2,32,384]{3,2,1,0:T(8,128)(2,1)S(1)}, u32[]{:S(2)}, u32[]{:S(2)}) %all-to-all-start) | async-done | bytes 786464 | tf_op jit(solution)/shard_map/all_to_all | solution.py:308
  89.4 0.1 reduce_sum.12
  89.5 4.6 %collective-permute-start.14 = (bf16[2,32,384]{2,1,0:T(8,128)(2,1)S(1)}, bf16[2,32,384]{2,1,0:T(8,128)(2,1)S(1)}, u32[]{:S(2)}, u32[]{:S(2)}) collective-permute-start(bf16[2,32,384]{2,1,0:T(8,128)(2,1)S(1)} %reduce_sum.12), channel_id=1, source_target_pairs={{0,0},{2,32},{4,64},{6,96},{8,8},{10,40},{12,72},{14,104},{16,16},... | collective-permute-start | bytes 147464 | tf_op jit(solution)/shard_map/ppermute | solution.py:290
  94.1 0.9 broadcast_select_fusion
  95.1 4.3 %collective-permute-done.14 = bf16[2,32,384]{2,1,0:T(8,128)(2,1)S(1)} collective-permute-done((bf16[2,32,384]{2,1,0:T(8,128)(2,1)S(1)}, bf16[2,32,384]{2,1,0:T(8,128)(2,1)S(1)}, u32[]{:S(2)}, u32[]{:S(2)}) %collective-permute-start.14) | collective-permute-done | bytes 49184 | tf_op jit(solution)/shard_map/ppermute | solution.py:290
  99.4 0.6 slice_bitcast_fusion
  (39 shorter events, 0.3 us)
Async XLA Ops:
  0.6 1.9 %copy-start.8 = (bf16[384,32]{0,1:T(8,128)(2,1)S(1)}, bf16[384,32]{0,1:T(8,128)(2,1)}, u32[]{:S(2)}) copy-start(bf16[384,32]{0,1:T(8,128)(2,1)} %param.12) | copy-start | bytes 73732
  0.6 1.9 %copy-start.9 = (bf16[384,32]{0,1:T(8,128)(2,1)S(1)}, bf16[384,32]{0,1:T(8,128)(2,1)}, u32[]{:S(2)}) copy-start(bf16[384,32]{0,1:T(8,128)(2,1)} %param.11) | copy-start | bytes 73732
  2.5 31.2 %collective-permute-start.11 = (bf16[3,192,1024]{2,1,0:T(8,128)(2,1)S(1)}, bf16[3,192,1024]{2,1,0:T(8,128)(2,1)S(1)}, u32[]{:S(2)}, u32[]{:S(2)}) collective-permute-start(bf16[3,192,1024]{2,1,0:T(8,128)(2,1)S(1)} %maximum_select_fusion), channel_id=1, source_target_pairs={{0,8},{8,0},{1,9},{9,1},{2,10},{10,2},{3,11},{11,3},{4,12},{12,4},... | collective-permute-start | bytes 3538952 | tf_op jit(solution)/shard_map/ppermute | solution.py:294
  2.6 11.7 %collective-permute-start.3 = (bf16[2,32,384]{2,1,0:T(8,128)(2,1)S(1)}, bf16[2,32,384]{2,1,0:T(8,128)(2,1)S(1)}, u32[]{:S(2)}, u32[]{:S(2)}) collective-permute-start(bf16[2,32,384]{2,1,0:T(8,128)(2,1)S(1)} %pad_maximum_fusion.1), channel_id=1, source_target_pairs={{0,96},{2,0},{4,32},{6,64},{8,104},{10,8},{12,40},{14,72},{16,112}... | collective-permute-start | bytes 147464 | tf_op jit(solution)/shard_map/ppermute | solution.py:290
  6.5 7.8 %collective-permute-start.2 = (bf16[2,32,384]{2,1,0:T(8,128)(2,1)S(1)}, bf16[2,32,384]{2,1,0:T(8,128)(2,1)S(1)}, u32[]{:S(2)}, u32[]{:S(2)}) collective-permute-start(bf16[2,32,384]{2,1,0:T(8,128)(2,1)S(1)} %pad_maximum_fusion.1), channel_id=1, source_target_pairs={{0,64},{2,96},{4,0},{6,32},{8,72},{10,104},{12,8},{14,40},{16,80},... | collective-permute-start | bytes 147464 | tf_op jit(solution)/shard_map/ppermute | solution.py:290
  6.5 7.8 %collective-permute-start.1 = (bf16[2,32,384]{2,1,0:T(8,128)(2,1)S(1)}, bf16[2,32,384]{2,1,0:T(8,128)(2,1)S(1)}, u32[]{:S(2)}, u32[]{:S(2)}) collective-permute-start(bf16[2,32,384]{2,1,0:T(8,128)(2,1)S(1)} %pad_maximum_fusion.1), channel_id=1, source_target_pairs={{0,32},{2,64},{4,96},{6,0},{8,40},{10,72},{12,104},{14,8},{16,48},... | collective-permute-start | bytes 147464 | tf_op jit(solution)/shard_map/ppermute | solution.py:290
  6.6 10.1 %collective-permute-start = (bf16[2,32,384]{2,1,0:T(8,128)(2,1)S(1)}, bf16[2,32,384]{2,1,0:T(8,128)(2,1)S(1)}, u32[]{:S(2)}, u32[]{:S(2)}) collective-permute-start(bf16[2,32,384]{2,1,0:T(8,128)(2,1)S(1)} %pad_maximum_fusion.1), channel_id=1, source_target_pairs={{0,0},{2,32},{4,64},{6,96},{8,8},{10,40},{12,72},{14,104},{16,16},... | collective-permute-start | bytes 147464 | tf_op jit(solution)/shard_map/ppermute | solution.py:290
  16.8 16.8 %copy-start.1 = (bf16[4,2,32,384]{3,2,1,0:T(8,128)(2,1)}, bf16[4,2,32,384]{3,2,1,0:T(8,128)(2,1)S(1)}, u32[]{:S(2)}) copy-start(bf16[4,2,32,384]{3,2,1,0:T(8,128)(2,1)S(1)} %pad_maximum_fusion.refs_0_) | copy-start | bytes 589828
  16.8 11.8 %collective-permute-start.6 = (bf16[4,2,32,384]{3,2,1,0:T(8,128)(2,1)S(1)}, bf16[4,2,32,384]{3,2,1,0:T(8,128)(2,1)S(1)}, u32[]{:S(2)}, u32[]{:S(2)}) collective-permute-start(bf16[4,2,32,384]{3,2,1,0:T(8,128)(2,1)S(1)} %pad_maximum_fusion.refs_0_), channel_id=1, source_target_pairs={{0,17},{2,19},{4,21},{6,23},{8,25},{10,27},{12,29},{14,31},{16,0},... | collective-permute-start | bytes 589832 | tf_op jit(solution)/shard_map/ppermute | solution.py:290
  20.9 9.3 %collective-permute-start.5 = (bf16[4,2,32,384]{3,2,1,0:T(8,128)(2,1)S(1)}, bf16[4,2,32,384]{3,2,1,0:T(8,128)(2,1)S(1)}, u32[]{:S(2)}, u32[]{:S(2)}) collective-permute-start(bf16[4,2,32,384]{3,2,1,0:T(8,128)(2,1)S(1)} %pad_maximum_fusion.refs_0_), channel_id=1, source_target_pairs={{0,1},{2,3},{4,5},{6,7},{8,9},{10,11},{12,13},{14,15},{16,17},{18,... | collective-permute-start | bytes 589832 | tf_op jit(solution)/shard_map/ppermute | solution.py:290
  20.9 11.1 %collective-permute-start.4 = (bf16[4,2,32,384]{3,2,1,0:T(8,128)(2,1)S(1)}, bf16[4,2,32,384]{3,2,1,0:T(8,128)(2,1)S(1)}, u32[]{:S(2)}, u32[]{:S(2)}) collective-permute-start(bf16[4,2,32,384]{3,2,1,0:T(8,128)(2,1)S(1)} %pad_maximum_fusion.refs_0_), channel_id=1, source_target_pairs={{0,16},{2,18},{4,20},{6,22},{8,24},{10,26},{12,28},{14,30},{16,1},... | collective-permute-start | bytes 589832 | tf_op jit(solution)/shard_map/ppermute | solution.py:290
  22.2 10.5 %collective-permute-start.7 = (bf16[4,2,32,384]{3,2,1,0:T(8,128)(2,1)S(1)}, bf16[4,2,32,384]{3,2,1,0:T(8,128)(2,1)S(1)}, u32[]{:S(2)}, u32[]{:S(2)}) collective-permute-start(bf16[4,2,32,384]{3,2,1,0:T(8,128)(2,1)S(1)} %pad_maximum_fusion.refs_0_), channel_id=1, source_target_pairs={{0,8},{8,0},{1,9},{9,1},{2,10},{10,2},{3,11},{11,3},{4,12},{12,4},... | collective-permute-start | bytes 589832 | tf_op jit(solution)/shard_map/ppermute | solution.py:294
  28.7 5.0 %copy-start.3 = (bf16[4,2,32,384]{3,2,1,0:T(8,128)(2,1)}, bf16[4,2,32,384]{3,2,1,0:T(8,128)(2,1)S(1)}, u32[]{:S(2)}) copy-start(bf16[4,2,32,384]{3,2,1,0:T(8,128)(2,1)S(1)} %collective-permute-done.6.refs_3_) | copy-start | bytes 589828
  28.7 4.0 %collective-permute-start.10 = (bf16[4,2,32,384]{3,2,1,0:T(8,128)(2,1)S(1)}, bf16[4,2,32,384]{3,2,1,0:T(8,128)(2,1)S(1)}, u32[]{:S(2)}, u32[]{:S(2)}) collective-permute-start(bf16[4,2,32,384]{3,2,1,0:T(8,128)(2,1)S(1)} %collective-permute-done.6.refs_3_), channel_id=1, source_target_pairs={{0,8},{8,0},{1,9},{9,1},{2,10},{10,2},{3,11},{11,3},{4,12},{12,4},... | collective-permute-start | bytes 589832 | tf_op jit(solution)/shard_map/ppermute | solution.py:294
  30.3 3.4 %copy-start.4 = (bf16[4,2,32,384]{3,2,1,0:T(8,128)(2,1)}, bf16[4,2,32,384]{3,2,1,0:T(8,128)(2,1)S(1)}, u32[]{:S(2)}) copy-start(bf16[4,2,32,384]{3,2,1,0:T(8,128)(2,1)S(1)} %collective-permute-done.5.refs_2_) | copy-start | bytes 589828
  30.3 2.4 %collective-permute-start.9 = (bf16[4,2,32,384]{3,2,1,0:T(8,128)(2,1)S(1)}, bf16[4,2,32,384]{3,2,1,0:T(8,128)(2,1)}, u32[]{:S(2)}, u32[]{:S(2)}) collective-permute-start(bf16[4,2,32,384]{3,2,1,0:T(8,128)(2,1)S(1)} %collective-permute-done.5.refs_2_), channel_id=1, source_target_pairs={{0,8},{8,0},{1,9},{9,1},{2,10},{10,2},{3,11},{11,3},{4,12},{12,4},... | collective-permute-start | bytes 589832 | tf_op jit(solution)/shard_map/ppermute | solution.py:294
  32.1 1.6 %copy-start.5 = (bf16[4,2,32,384]{3,2,1,0:T(8,128)(2,1)}, bf16[4,2,32,384]{3,2,1,0:T(8,128)(2,1)S(1)}, u32[]{:S(2)}) copy-start(bf16[4,2,32,384]{3,2,1,0:T(8,128)(2,1)S(1)} %collective-permute-done.4.refs_1_) | copy-start | bytes 589828
  32.1 1.6 %collective-permute-start.8 = (bf16[4,2,32,384]{3,2,1,0:T(8,128)(2,1)S(1)}, bf16[4,2,32,384]{3,2,1,0:T(8,128)(2,1)}, u32[]{:S(2)}, u32[]{:S(2)}) collective-permute-start(bf16[4,2,32,384]{3,2,1,0:T(8,128)(2,1)S(1)} %collective-permute-done.4.refs_1_), channel_id=1, source_target_pairs={{0,8},{8,0},{1,9},{9,1},{2,10},{10,2},{3,11},{11,3},{4,12},{12,4},... | collective-permute-start | bytes 589832 | tf_op jit(solution)/shard_map/ppermute | solution.py:294
  66.2 2.6 %collective-permute-start.13 = (bf16[16,2,32,384]{3,2,1,0:T(8,128)(2,1)}, bf16[16,2,32,384]{3,2,1,0:T(8,128)(2,1)S(1)}, u32[]{:S(2)}, u32[]{:S(2)}) collective-permute-start(bf16[16,2,32,384]{3,2,1,0:T(8,128)(2,1)} %get-tuple-element.11), channel_id=1, source_target_pairs={{0,8},{8,0},{1,9},{9,1},{2,10},{10,2},{3,11},{11,3},{4,12},{12,4},... | collective-permute-start | bytes 2359304 | tf_op jit(solution)/shard_map/ppermute | solution.py:294
  71.0 5.0 %copy-start.10 = (bf16[192,1024]{1,0:T(8,128)(2,1)S(1)}, bf16[192,1024]{1,0:T(8,128)(2,1)}, u32[]{:S(2)}) copy-start(bf16[192,1024]{1,0:T(8,128)(2,1)} %get-tuple-element.9) | copy-start | bytes 1179652
  71.0 23.1 %copy-start.2 = (bf16[192,1024]{1,0:T(8,128)(2,1)S(1)}, bf16[192,1024]{1,0:T(8,128)(2,1)}, u32[]{:S(2)}) copy-start(bf16[192,1024]{1,0:T(8,128)(2,1)} %get-tuple-element.8) | copy-start | bytes 1179652
  71.0 18.4 %all-to-all-start = ((bf16[16,2,32,384]{3,2,1,0:T(8,128)(2,1)}), bf16[16,2,32,384]{3,2,1,0:T(8,128)(2,1)S(1)}, u32[]{:S(2)}, u32[]{:S(2)}) async-start(bf16[16,2,32,384]{3,2,1,0:T(8,128)(2,1)} %add_convert_fusion), calls=%async_computation | async-start | bytes 1572864 | tf_op jit(solution)/shard_map/all_to_all | solution.py:308
  76.0 18.1 %collective-permute-start.12 = (bf16[192,1024]{1,0:T(8,128)(2,1)S(1)}, bf16[192,1024]{1,0:T(8,128)(2,1)S(1)}, u32[]{:S(2)}, u32[]{:S(2)}) collective-permute-start(bf16[192,1024]{1,0:T(8,128)(2,1)S(1)} %copy-done.10), channel_id=1, source_target_pairs={{0,8},{8,0},{1,9},{9,1},{2,10},{10,2},{3,11},{11,3},{4,12},{12,4},... | collective-permute-start | bytes 1179656 | tf_op jit(solution)/shard_map/ppermute | solution.py:294
  89.5 9.9 %collective-permute-start.14 = (bf16[2,32,384]{2,1,0:T(8,128)(2,1)S(1)}, bf16[2,32,384]{2,1,0:T(8,128)(2,1)S(1)}, u32[]{:S(2)}, u32[]{:S(2)}) collective-permute-start(bf16[2,32,384]{2,1,0:T(8,128)(2,1)S(1)} %reduce_sum.12), channel_id=1, source_target_pairs={{0,0},{2,32},{4,64},{6,96},{8,8},{10,40},{12,72},{14,104},{16,16},... | collective-permute-start | bytes 147464 | tf_op jit(solution)/shard_map/ppermute | solution.py:290
  (3 other events, 3.1 us)

commit v2 on v1

--- a/solution.py
+++ b/solution.py
@@ -73,9 +73,9 @@
                 for i in range(3):
                     own_copy(i, layer).start()
 
-        other_copy().start()
         for i in range(8):
             piece_copy(i).wait()
+        other_copy().start()
         for which in range(2):
             for side in range(2):
                 core_at = core if side == 0 else 1 - core
@@ -229,7 +229,6 @@
     lanes = heads * BLK
     piece = pieces[0].shape
     keys = 8 * piece[-1]
-    whole = lambda shape: pl.BlockSpec(shape, lambda i, *s: (0,) * len(shape))
     first = lambda i: jnp.minimum(i, half - 1)
     second = lambda i: jnp.maximum(i - half, 0)
     rows = (BLK, heads * HEAD)
@@ -244,8 +243,8 @@
             out_specs=[
                 pl.BlockSpec(rows, lambda i, *s: (first(i), 0)),
                 pl.BlockSpec(rows, lambda i, *s: (second(i), 0)),
-                whole(parts),
-                whole(parts),
+                pl.BlockSpec(memory_space=pltpu.VMEM),
+                pl.BlockSpec(memory_space=pltpu.VMEM),
             ],
             scratch_shapes=[
                 pltpu.VMEM((HEAD, keys), F32),
@@ -268,8 +267,8 @@
         out_shape=[
             gradient,
             gradient,
-            jax.ShapeDtypeStruct(parts, BF16),
-            jax.ShapeDtypeStruct(parts, BF16),
+            pltpu.VMEM(parts, BF16),
+            pltpu.VMEM(parts, BF16),
         ],
         compiler_params=pltpu.CompilerParams(vmem_limit_bytes=56 * 1024 * 1024),
         name="attention",

time: 101 us -> 101 us (level)
  Pallas kernels: 31.4 us -> 28.4 us
  starting transfers between devices: 27.1 us -> 29.4 us
  waiting for transfers between devices: 33.2 us -> 35.2 us
  other arithmetic: 5.77 us -> 4.69 us
    all_to_all x1, starting transfers between devices: 4.96 us -> 9.51 us  [reduce_pieces(): parts = lax.all_to_all(chip, ('x', 'zl', 'zh'), 0, 0)]
    pallas_call x1, Pallas kernels: 31.4 us -> 28.4 us  [attention(): pl.pallas_call(attention_kernel, grid_spec=pltpu.PrefetchScalarGridSpec(n...]
    ppermute x8, waiting for transfers between devices: 16.7 us -> 19 us  [moved(): return lax.ppermute(value, AXES, pairs)]
    ppermute x8, starting transfers between devices: 21.6 us -> 19.3 us  [moved(): return lax.ppermute(value, AXES, pairs)]
    convert_element_type x1, other arithmetic: 2.26 us -> 1.13 us  [reduce_pieces(): chip = (keep.astype(F32) + swap_cores(give).astype(F32)).astype(BF16)]
where the time goes in v2:
time: 101 us; the launch traced here: 100 us
  waiting for transfers between devices  35.2 us (35%)
  starting transfers between devices  29.4 us (29%)
  Pallas kernels  28.4 us (28%)
  other arithmetic  4.69 us (5%)
  local copies, waits for them, and re-layouts  1.7 us (2%)
    pallas_call x1, Pallas kernels, attention(): pl.pallas_call(attention_kernel, grid_spec=pltpu.PrefetchScalarGridSpec(n...  28.4 us
    ppermute x8, starting transfers between devices, moved(): return lax.ppermute(value, AXES, pairs)  19.3 us
    ppermute x8, waiting for transfers between devices, moved(): return lax.ppermute(value, AXES, pairs)  19 us
    all_to_all x1, waiting for transfers between devices, reduce_pieces(): parts = lax.all_to_all(chip, ('x', 'zl', 'zh'), 0, 0)  13.4 us
    all_to_all x1, starting transfers between devices, reduce_pieces(): parts = lax.all_to_all(chip, ('x', 'zl', 'zh'), 0, 0)  9.51 us
    ppermute x7, waiting for transfers between devices, swap_cores(): return lax.ppermute(value, 'core', [(0, 1), (1, 0)])  2.86 us
  transfers between devices with their start and end apart: 16, of which 8 were waited for; matrix products, arithmetic and copies ran while one was open for 2% of the time, Pallas kernels for 0%

profile of v2, /device:TPU:4, one launch (start us, length us, event | category | flops | bytes accessed | tf_op | source)
XLA Modules:
  0.0 100.3 jit_solution(458240643165192059)
XLA Ops:
  0.7 1.8 %maximum_select_fusion = bf16[3,192,1024]{2,1,0:T(8,128)(2,1)S(1)} fusion(bf16[1,192,1024]{2,1,0:T(8,128)(2,1)} %bitcast.32, bf16[1,192,1024]{2,1,0:T(8,128)(2,1)} %bitcast.30, bf16[1,192,1024]{2,1,0:T(8,128)(2,1)} %bitcast.28, bf16[1,192,1024]{2,1,0:T(8,128)(2,1)} %bitcast.31, bf16[1,192,1024]{2,1,0:T(8,128)(2,1)} %bitcast.29, ...), kind=kLoop, calls=%fused_computation.1 | loop fusion | flops 2949120 | bytes 3538945 | tf_op jit(solution)/shard_map/jit(_where)/select_n | solution.py:317
  2.6 3.9 %collective-permute-start.3 = (bf16[2,32,384]{2,1,0:T(8,128)(2,1)S(1)}, bf16[2,32,384]{2,1,0:T(8,128)(2,1)S(1)}, u32[]{:S(2)}, u32[]{:S(2)}) collective-permute-start(bf16[2,32,384]{2,1,0:T(8,128)(2,1)S(1)} %pad_maximum_fusion.1), channel_id=1, source_target_pairs={{0,96},{2,0},{4,32},{6,64},{8,104},{10,8},{12,40},{14,72},{16,112}... | collective-permute-start | bytes 147464 | tf_op jit(solution)/shard_map/ppermute | solution.py:289
  6.5 0.1 collective-permute-start.1
  6.6 7.6 %collective-permute-start = (bf16[2,32,384]{2,1,0:T(8,128)(2,1)S(1)}, bf16[2,32,384]{2,1,0:T(8,128)(2,1)S(1)}, u32[]{:S(2)}, u32[]{:S(2)}) collective-permute-start(bf16[2,32,384]{2,1,0:T(8,128)(2,1)S(1)} %pad_maximum_fusion.1), channel_id=1, source_target_pairs={{0,0},{2,32},{4,64},{6,96},{8,8},{10,40},{12,72},{14,104},{16,16},... | collective-permute-start | bytes 147464 | tf_op jit(solution)/shard_map/ppermute | solution.py:289
  14.3 2.5 %collective-permute-done = bf16[2,32,384]{2,1,0:T(8,128)(2,1)S(1)} collective-permute-done((bf16[2,32,384]{2,1,0:T(8,128)(2,1)S(1)}, bf16[2,32,384]{2,1,0:T(8,128)(2,1)S(1)}, u32[]{:S(2)}, u32[]{:S(2)}) %collective-permute-start) | collective-permute-done | bytes 49184 | tf_op jit(solution)/shard_map/ppermute | solution.py:289
  16.8 4.1 %collective-permute-start.6 = (bf16[4,2,32,384]{3,2,1,0:T(8,128)(2,1)S(1)}, bf16[4,2,32,384]{3,2,1,0:T(8,128)(2,1)S(1)}, u32[]{:S(2)}, u32[]{:S(2)}) collective-permute-start(bf16[4,2,32,384]{3,2,1,0:T(8,128)(2,1)S(1)} %pad_maximum_fusion.refs_0_), channel_id=1, source_target_pairs={{0,17},{2,19},{4,21},{6,23},{8,25},{10,27},{12,29},{14,31},{16,0},... | collective-permute-start | bytes 589832 | tf_op jit(solution)/shard_map/ppermute | solution.py:289
  20.9 1.3 %collective-permute-start.4 = (bf16[4,2,32,384]{3,2,1,0:T(8,128)(2,1)S(1)}, bf16[4,2,32,384]{3,2,1,0:T(8,128)(2,1)S(1)}, u32[]{:S(2)}, u32[]{:S(2)}) collective-permute-start(bf16[4,2,32,384]{3,2,1,0:T(8,128)(2,1)S(1)} %pad_maximum_fusion.refs_0_), channel_id=1, source_target_pairs={{0,16},{2,18},{4,20},{6,22},{8,24},{10,26},{12,28},{14,30},{16,1},... | collective-permute-start | bytes 589832 | tf_op jit(solution)/shard_map/ppermute | solution.py:289
  22.2 6.5 %collective-permute-done.6.refs_3_ = bf16[4,2,32,384]{3,2,1,0:T(8,128)(2,1)S(1)} collective-permute-done((bf16[4,2,32,384]{3,2,1,0:T(8,128)(2,1)S(1)}, bf16[4,2,32,384]{3,2,1,0:T(8,128)(2,1)S(1)}, u32[]{:S(2)}, u32[]{:S(2)}) %collective-permute-start.6) | collective-permute-done | bytes 196640 | tf_op jit(solution)/shard_map/ppermute | solution.py:289
  28.7 1.6 %collective-permute-done.5.refs_2_ = bf16[4,2,32,384]{3,2,1,0:T(8,128)(2,1)S(1)} collective-permute-done((bf16[4,2,32,384]{3,2,1,0:T(8,128)(2,1)S(1)}, bf16[4,2,32,384]{3,2,1,0:T(8,128)(2,1)S(1)}, u32[]{:S(2)}, u32[]{:S(2)}) %collective-permute-start.5) | collective-permute-done | bytes 196640 | tf_op jit(solution)/shard_map/ppermute | solution.py:289
  30.3 1.8 %collective-permute-done.4.refs_1_ = bf16[4,2,32,384]{3,2,1,0:T(8,128)(2,1)S(1)} collective-permute-done((bf16[4,2,32,384]{3,2,1,0:T(8,128)(2,1)S(1)}, bf16[4,2,32,384]{3,2,1,0:T(8,128)(2,1)S(1)}, u32[]{:S(2)}, u32[]{:S(2)}) %collective-permute-start.4) | collective-permute-done | bytes 196640 | tf_op jit(solution)/shard_map/ppermute | solution.py:289
  32.1 0.6 pad_add_fusion.place_ref
  32.8 0.9 collective-permute-done.8.refs_5_
  33.7 1.0 %copy-done = bf16[3,192,1024]{2,1,0:T(8,128)(2,1)} copy-done((bf16[3,192,1024]{2,1,0:T(8,128)(2,1)}, bf16[3,192,1024]{2,1,0:T(8,128)(2,1)S(1)}, u32[]{:S(2)}) %copy-start) | copy-done | bytes 1179672
  34.7 28.4 %attention.1 = (bf16[192,1024]{1,0:T(8,128)(2,1)}, bf16[192,1024]{1,0:T(8,128)(2,1)}, bf16[16,2,32,384]{3,2,1,0:T(8,128)(2,1)S(1)}, bf16[16,2,32,384]{3,2,1,0:T(8,128)(2,1)S(1)}) custom-call(s32[48]{0:T(128)} %order_ref.1, s32[3]{0:T(128)} %pad_add_fusion.place_ref, bf16[4,2,32,384]{3,2,1,0:T(8,128)(2,1)} %copy-done.1, bf16[4,2,32,384]{3,2,1,0:T(8,128)(2,1)} %copy-done.5, ...), custom_call_target="tpu_custom_call" | custom-call | tf_op jit(solution)/shard_map/attention/pallas_call | solution.py:237
  63.2 0.4 collective-permute-start.13
  63.6 2.0 %collective-permute-done.13 = bf16[16,2,32,384]{3,2,1,0:T(8,128)(2,1)S(1)} collective-permute-done((bf16[16,2,32,384]{3,2,1,0:T(8,128)(2,1)S(1)}, bf16[16,2,32,384]{3,2,1,0:T(8,128)(2,1)S(1)}, u32[]{:S(2)}, u32[]{:S(2)}) %collective-permute-start.13) | collective-permute-done | bytes 786464 | tf_op jit(solution)/shard_map/ppermute | solution.py:293
  65.5 1.1 %add_convert_fusion = bf16[16,2,32,384]{3,2,1,0:T(8,128)(2,1)} fusion(bf16[16,2,32,384]{3,2,1,0:T(8,128)(2,1)S(1)} %collective-permute-done.13, bf16[16,2,32,384]{3,2,1,0:T(8,128)(2,1)S(1)} %get-tuple-element.10), kind=kLoop, calls=%fused_computation | loop fusion | flops 1572864 | bytes 2359296 | tf_op jit(solution)/shard_map/convert_element_type | solution.py:306
  66.7 9.5 %all-to-all-start = ((bf16[16,2,32,384]{3,2,1,0:T(8,128)(2,1)}), bf16[16,2,32,384]{3,2,1,0:T(8,128)(2,1)S(1)}, u32[]{:S(2)}, u32[]{:S(2)}) async-start(bf16[16,2,32,384]{3,2,1,0:T(8,128)(2,1)} %add_convert_fusion), calls=%async_computation | async-start | bytes 1572864 | tf_op jit(solution)/shard_map/all_to_all | solution.py:307
  76.3 13.4 %all-to-all-done = bf16[16,2,32,384]{3,2,1,0:T(8,128)(2,1)S(1)} async-done(((bf16[16,2,32,384]{3,2,1,0:T(8,128)(2,1)}), bf16[16,2,32,384]{3,2,1,0:T(8,128)(2,1)S(1)}, u32[]{:S(2)}, u32[]{:S(2)}) %all-to-all-start) | async-done | bytes 786464 | tf_op jit(solution)/shard_map/all_to_all | solution.py:307
  89.6 0.1 reduce_sum.12
  89.8 2.3 %collective-permute-start.14 = (bf16[2,32,384]{2,1,0:T(8,128)(2,1)S(1)}, bf16[2,32,384]{2,1,0:T(8,128)(2,1)S(1)}, u32[]{:S(2)}, u32[]{:S(2)}) collective-permute-start(bf16[2,32,384]{2,1,0:T(8,128)(2,1)S(1)} %reduce_sum.12), channel_id=1, source_target_pairs={{0,0},{2,32},{4,64},{6,96},{8,8},{10,40},{12,72},{14,104},{16,16},... | collective-permute-start | bytes 147464 | tf_op jit(solution)/shard_map/ppermute | solution.py:289
  92.0 0.9 broadcast_select_fusion
  93.0 6.7 %collective-permute-done.14 = bf16[2,32,384]{2,1,0:T(8,128)(2,1)S(1)} collective-permute-done((bf16[2,32,384]{2,1,0:T(8,128)(2,1)S(1)}, bf16[2,32,384]{2,1,0:T(8,128)(2,1)S(1)}, u32[]{:S(2)}, u32[]{:S(2)}) %collective-permute-start.14) | collective-permute-done | bytes 49184 | tf_op jit(solution)/shard_map/ppermute | solution.py:289
  99.7 0.6 slice_bitcast_fusion
  (39 shorter events, 0.3 us)
Async XLA Ops:
  0.6 1.9 %copy-start.8 = (bf16[384,32]{0,1:T(8,128)(2,1)S(1)}, bf16[384,32]{0,1:T(8,128)(2,1)}, u32[]{:S(2)}) copy-start(bf16[384,32]{0,1:T(8,128)(2,1)} %param.12) | copy-start | bytes 73732
  0.6 1.9 %copy-start.9 = (bf16[384,32]{0,1:T(8,128)(2,1)S(1)}, bf16[384,32]{0,1:T(8,128)(2,1)}, u32[]{:S(2)}) copy-start(bf16[384,32]{0,1:T(8,128)(2,1)} %param.11) | copy-start | bytes 73732
  2.5 31.2 %collective-permute-start.11 = (bf16[3,192,1024]{2,1,0:T(8,128)(2,1)S(1)}, bf16[3,192,1024]{2,1,0:T(8,128)(2,1)S(1)}, u32[]{:S(2)}, u32[]{:S(2)}) collective-permute-start(bf16[3,192,1024]{2,1,0:T(8,128)(2,1)S(1)} %maximum_select_fusion), channel_id=1, source_target_pairs={{0,8},{8,0},{1,9},{9,1},{2,10},{10,2},{3,11},{11,3},{4,12},{12,4},... | collective-permute-start | bytes 3538952 | tf_op jit(solution)/shard_map/ppermute | solution.py:293
  2.6 11.7 %collective-permute-start.3 = (bf16[2,32,384]{2,1,0:T(8,128)(2,1)S(1)}, bf16[2,32,384]{2,1,0:T(8,128)(2,1)S(1)}, u32[]{:S(2)}, u32[]{:S(2)}) collective-permute-start(bf16[2,32,384]{2,1,0:T(8,128)(2,1)S(1)} %pad_maximum_fusion.1), channel_id=1, source_target_pairs={{0,96},{2,0},{4,32},{6,64},{8,104},{10,8},{12,40},{14,72},{16,112}... | collective-permute-start | bytes 147464 | tf_op jit(solution)/shard_map/ppermute | solution.py:289
  6.5 7.8 %collective-permute-start.2 = (bf16[2,32,384]{2,1,0:T(8,128)(2,1)S(1)}, bf16[2,32,384]{2,1,0:T(8,128)(2,1)S(1)}, u32[]{:S(2)}, u32[]{:S(2)}) collective-permute-start(bf16[2,32,384]{2,1,0:T(8,128)(2,1)S(1)} %pad_maximum_fusion.1), channel_id=1, source_target_pairs={{0,64},{2,96},{4,0},{6,32},{8,72},{10,104},{12,8},{14,40},{16,80},... | collective-permute-start | bytes 147464 | tf_op jit(solution)/shard_map/ppermute | solution.py:289
  6.5 7.8 %collective-permute-start.1 = (bf16[2,32,384]{2,1,0:T(8,128)(2,1)S(1)}, bf16[2,32,384]{2,1,0:T(8,128)(2,1)S(1)}, u32[]{:S(2)}, u32[]{:S(2)}) collective-permute-start(bf16[2,32,384]{2,1,0:T(8,128)(2,1)S(1)} %pad_maximum_fusion.1), channel_id=1, source_target_pairs={{0,32},{2,64},{4,96},{6,0},{8,40},{10,72},{12,104},{14,8},{16,48},... | collective-permute-start | bytes 147464 | tf_op jit(solution)/shard_map/ppermute | solution.py:289
  6.6 10.1 %collective-permute-start = (bf16[2,32,384]{2,1,0:T(8,128)(2,1)S(1)}, bf16[2,32,384]{2,1,0:T(8,128)(2,1)S(1)}, u32[]{:S(2)}, u32[]{:S(2)}) collective-permute-start(bf16[2,32,384]{2,1,0:T(8,128)(2,1)S(1)} %pad_maximum_fusion.1), channel_id=1, source_target_pairs={{0,0},{2,32},{4,64},{6,96},{8,8},{10,40},{12,72},{14,104},{16,16},... | collective-permute-start | bytes 147464 | tf_op jit(solution)/shard_map/ppermute | solution.py:289
  16.8 16.8 %copy-start.1 = (bf16[4,2,32,384]{3,2,1,0:T(8,128)(2,1)}, bf16[4,2,32,384]{3,2,1,0:T(8,128)(2,1)S(1)}, u32[]{:S(2)}) copy-start(bf16[4,2,32,384]{3,2,1,0:T(8,128)(2,1)S(1)} %pad_maximum_fusion.refs_0_) | copy-start | bytes 589828
  16.8 11.8 %collective-permute-start.6 = (bf16[4,2,32,384]{3,2,1,0:T(8,128)(2,1)S(1)}, bf16[4,2,32,384]{3,2,1,0:T(8,128)(2,1)S(1)}, u32[]{:S(2)}, u32[]{:S(2)}) collective-permute-start(bf16[4,2,32,384]{3,2,1,0:T(8,128)(2,1)S(1)} %pad_maximum_fusion.refs_0_), channel_id=1, source_target_pairs={{0,17},{2,19},{4,21},{6,23},{8,25},{10,27},{12,29},{14,31},{16,0},... | collective-permute-start | bytes 589832 | tf_op jit(solution)/shard_map/ppermute | solution.py:289
  20.9 9.3 %collective-permute-start.5 = (bf16[4,2,32,384]{3,2,1,0:T(8,128)(2,1)S(1)}, bf16[4,2,32,384]{3,2,1,0:T(8,128)(2,1)S(1)}, u32[]{:S(2)}, u32[]{:S(2)}) collective-permute-start(bf16[4,2,32,384]{3,2,1,0:T(8,128)(2,1)S(1)} %pad_maximum_fusion.refs_0_), channel_id=1, source_target_pairs={{0,1},{2,3},{4,5},{6,7},{8,9},{10,11},{12,13},{14,15},{16,17},{18,... | collective-permute-start | bytes 589832 | tf_op jit(solution)/shard_map/ppermute | solution.py:289
  20.9 11.1 %collective-permute-start.4 = (bf16[4,2,32,384]{3,2,1,0:T(8,128)(2,1)S(1)}, bf16[4,2,32,384]{3,2,1,0:T(8,128)(2,1)S(1)}, u32[]{:S(2)}, u32[]{:S(2)}) collective-permute-start(bf16[4,2,32,384]{3,2,1,0:T(8,128)(2,1)S(1)} %pad_maximum_fusion.refs_0_), channel_id=1, source_target_pairs={{0,16},{2,18},{4,20},{6,22},{8,24},{10,26},{12,28},{14,30},{16,1},... | collective-permute-start | bytes 589832 | tf_op jit(solution)/shard_map/ppermute | solution.py:289
  22.2 10.5 %collective-permute-start.7 = (bf16[4,2,32,384]{3,2,1,0:T(8,128)(2,1)S(1)}, bf16[4,2,32,384]{3,2,1,0:T(8,128)(2,1)S(1)}, u32[]{:S(2)}, u32[]{:S(2)}) collective-permute-start(bf16[4,2,32,384]{3,2,1,0:T(8,128)(2,1)S(1)} %pad_maximum_fusion.refs_0_), channel_id=1, source_target_pairs={{0,8},{8,0},{1,9},{9,1},{2,10},{10,2},{3,11},{11,3},{4,12},{12,4},... | collective-permute-start | bytes 589832 | tf_op jit(solution)/shard_map/ppermute | solution.py:293
  28.7 5.0 %copy-start.3 = (bf16[4,2,32,384]{3,2,1,0:T(8,128)(2,1)}, bf16[4,2,32,384]{3,2,1,0:T(8,128)(2,1)S(1)}, u32[]{:S(2)}) copy-start(bf16[4,2,32,384]{3,2,1,0:T(8,128)(2,1)S(1)} %collective-permute-done.6.refs_3_) | copy-start | bytes 589828
  28.7 4.1 %collective-permute-start.10 = (bf16[4,2,32,384]{3,2,1,0:T(8,128)(2,1)S(1)}, bf16[4,2,32,384]{3,2,1,0:T(8,128)(2,1)S(1)}, u32[]{:S(2)}, u32[]{:S(2)}) collective-permute-start(bf16[4,2,32,384]{3,2,1,0:T(8,128)(2,1)S(1)} %collective-permute-done.6.refs_3_), channel_id=1, source_target_pairs={{0,8},{8,0},{1,9},{9,1},{2,10},{10,2},{3,11},{11,3},{4,12},{12,4},... | collective-permute-start | bytes 589832 | tf_op jit(solution)/shard_map/ppermute | solution.py:293
  30.3 3.4 %copy-start.4 = (bf16[4,2,32,384]{3,2,1,0:T(8,128)(2,1)}, bf16[4,2,32,384]{3,2,1,0:T(8,128)(2,1)S(1)}, u32[]{:S(2)}) copy-start(bf16[4,2,32,384]{3,2,1,0:T(8,128)(2,1)S(1)} %collective-permute-done.5.refs_2_) | copy-start | bytes 589828
  30.3 2.5 %collective-permute-start.9 = (bf16[4,2,32,384]{3,2,1,0:T(8,128)(2,1)S(1)}, bf16[4,2,32,384]{3,2,1,0:T(8,128)(2,1)}, u32[]{:S(2)}, u32[]{:S(2)}) collective-permute-start(bf16[4,2,32,384]{3,2,1,0:T(8,128)(2,1)S(1)} %collective-permute-done.5.refs_2_), channel_id=1, source_target_pairs={{0,8},{8,0},{1,9},{9,1},{2,10},{10,2},{3,11},{11,3},{4,12},{12,4},... | collective-permute-start | bytes 589832 | tf_op jit(solution)/shard_map/ppermute | solution.py:293
  32.1 1.6 %copy-start.5 = (bf16[4,2,32,384]{3,2,1,0:T(8,128)(2,1)}, bf16[4,2,32,384]{3,2,1,0:T(8,128)(2,1)S(1)}, u32[]{:S(2)}) copy-start(bf16[4,2,32,384]{3,2,1,0:T(8,128)(2,1)S(1)} %collective-permute-done.4.refs_1_) | copy-start | bytes 589828
  32.1 1.6 %collective-permute-start.8 = (bf16[4,2,32,384]{3,2,1,0:T(8,128)(2,1)S(1)}, bf16[4,2,32,384]{3,2,1,0:T(8,128)(2,1)}, u32[]{:S(2)}, u32[]{:S(2)}) collective-permute-start(bf16[4,2,32,384]{3,2,1,0:T(8,128)(2,1)S(1)} %collective-permute-done.4.refs_1_), channel_id=1, source_target_pairs={{0,8},{8,0},{1,9},{9,1},{2,10},{10,2},{3,11},{11,3},{4,12},{12,4},... | collective-permute-start | bytes 589832 | tf_op jit(solution)/shard_map/ppermute | solution.py:293
  63.2 2.4 %collective-permute-start.13 = (bf16[16,2,32,384]{3,2,1,0:T(8,128)(2,1)S(1)}, bf16[16,2,32,384]{3,2,1,0:T(8,128)(2,1)S(1)}, u32[]{:S(2)}, u32[]{:S(2)}) collective-permute-start(bf16[16,2,32,384]{3,2,1,0:T(8,128)(2,1)S(1)} %get-tuple-element.11), channel_id=1, source_target_pairs={{0,8},{8,0},{1,9},{9,1},{2,10},{10,2},{3,11},{11,3},{4,12},{12,4},... | collective-permute-start | bytes 2359304 | tf_op jit(solution)/shard_map/ppermute | solution.py:293
  66.7 9.5 %copy-start.10 = (bf16[192,1024]{1,0:T(8,128)(2,1)S(1)}, bf16[192,1024]{1,0:T(8,128)(2,1)}, u32[]{:S(2)}) copy-start(bf16[192,1024]{1,0:T(8,128)(2,1)} %get-tuple-element.9) | copy-start | bytes 1179652
  66.7 25.4 %copy-start.2 = (bf16[192,1024]{1,0:T(8,128)(2,1)S(1)}, bf16[192,1024]{1,0:T(8,128)(2,1)}, u32[]{:S(2)}) copy-start(bf16[192,1024]{1,0:T(8,128)(2,1)} %get-tuple-element.8) | copy-start | bytes 1179652
  66.7 23.0 %all-to-all-start = ((bf16[16,2,32,384]{3,2,1,0:T(8,128)(2,1)}), bf16[16,2,32,384]{3,2,1,0:T(8,128)(2,1)S(1)}, u32[]{:S(2)}, u32[]{:S(2)}) async-start(bf16[16,2,32,384]{3,2,1,0:T(8,128)(2,1)} %add_convert_fusion), calls=%async_computation | async-start | bytes 1572864 | tf_op jit(solution)/shard_map/all_to_all | solution.py:307
  76.2 15.8 %collective-permute-start.12 = (bf16[192,1024]{1,0:T(8,128)(2,1)S(1)}, bf16[192,1024]{1,0:T(8,128)(2,1)S(1)}, u32[]{:S(2)}, u32[]{:S(2)}) collective-permute-start(bf16[192,1024]{1,0:T(8,128)(2,1)S(1)} %copy-done.10), channel_id=1, source_target_pairs={{0,8},{8,0},{1,9},{9,1},{2,10},{10,2},{3,11},{11,3},{4,12},{12,4},... | collective-permute-start | bytes 1179656 | tf_op jit(solution)/shard_map/ppermute | solution.py:293
  89.8 9.9 %collective-permute-start.14 = (bf16[2,32,384]{2,1,0:T(8,128)(2,1)S(1)}, bf16[2,32,384]{2,1,0:T(8,128)(2,1)S(1)}, u32[]{:S(2)}, u32[]{:S(2)}) collective-permute-start(bf16[2,32,384]{2,1,0:T(8,128)(2,1)S(1)} %reduce_sum.12), channel_id=1, source_target_pairs={{0,0},{2,32},{4,64},{6,96},{8,8},{10,40},{12,72},{14,104},{16,16},... | collective-permute-start | bytes 147464 | tf_op jit(solution)/shard_map/ppermute | solution.py:289
  (3 other events, 3.0 us)

commit v3 on v2

--- a/solution.py
+++ b/solution.py
@@ -11,7 +11,7 @@
 HEAD = 128
 BLK = 64
 CHUNK = 256
-LADDER = (8, 4, 2, 1)
+LADDER = (6, 4, 3, 2, 1)
 SCALE = 1.0 / math.sqrt(HEAD)
 SCALE_LOG2 = SCALE * math.log2(math.e)
 NEG = -1e30
@@ -293,20 +293,35 @@
     return lax.ppermute(value, "core", [(0, 1), (1, 0)])
 
 
-def spread(piece):
+def spread(piece, other):
     parts = jnp.stack(
         [moved(piece, lambda x, z, core, y, d=d: ((y + d) % 4, z, core, x)) for d in range(4)]
     )
-    return [parts] + [
+    parts, other = lax.optimization_barrier((parts, other))
+    turns = [parts] + [
         moved(parts, lambda x, z, core, y, d=d: (x, (z + d) % 4, core, y)) for d in (1, 2, 3)
     ]
+    return turns, other
 
 
 def reduce_pieces(keep, give):
-    chip = (keep.astype(F32) + swap_cores(give).astype(F32)).astype(BF16)
-    parts = lax.all_to_all(chip, ("x", "zl", "zh"), 0, 0)
-    total = jnp.sum(parts.astype(F32), axis=0).astype(BF16)
-    return moved(total, lambda x, z, core, y: (y, z, core, x))
+    z = lax.axis_index("zh") * 2 + lax.axis_index("zl")
+    x = lax.axis_index("x")
+    chip = keep.astype(F32) + swap_cores(give).astype(F32)
+    chip = chip.reshape((4, 2, 2) + chip.shape[1:]).transpose(0, 2, 1, 3, 4, 5).reshape((4, 4) + chip.shape[1:])
+
+    def take(value, k, axis):
+        return lax.dynamic_index_in_dim(value, k % 4, axis, keepdims=False)
+
+    low = chip.astype(BF16)
+    total = take(low, z, 1).astype(F32)
+    for d in (1, 2, 3):
+        total = total + moved(take(low, z + d, 1), lambda x, z, core, y, d=d: (x, (z + d) % 4, core, y)).astype(F32)
+    low = total.astype(BF16)
+    return sum(
+        moved(take(low, x + d, 0), lambda x, z, core, y, d=d: (y, z, core, (x + d) % 4)).astype(F32)
+        for d in range(4)
+    ).astype(BF16)
 
 
 def per_device(q1, q2, keys, values, u1, u2, o1, o2, block_order):
@@ -315,7 +330,7 @@
     place = jnp.stack([core, x, z]).astype(jnp.int32)
     own = (q1, q2, u1, u2, o1, o2)
     other = swap_cores(jnp.where(core == 0, jnp.stack(own[1::2]), jnp.stack(own[::2])))
-    pieces = spread(jnp.stack([keys.T, values.T]))
+    pieces, other = spread(jnp.stack([keys.T, values.T]), other)
     pieces = pieces + [swap_cores(piece) for piece in pieces]
     dq_own, dq_other, keep, give = attention(block_order, place, pieces, (*own, other))
     dq_back = swap_cores(dq_other)

time: 101 us -> 94.6 us (0.937)
  waiting for transfers between devices: 35.2 us -> 29.2 us
  starting transfers between devices: 29.4 us -> 32.7 us
  Pallas kernels: 28.4 us -> 25.1 us
    all_to_all x1 -> x0, waiting for transfers between devices: 13.4 us -> none  [reduce_pieces(): parts = lax.all_to_all(chip, ('x', 'zl', 'zh'), 0, 0)]
    ppermute x8 -> x14, starting transfers between devices: 19.3 us -> 31.7 us  [moved(): return lax.ppermute(value, AXES, pairs)]
    all_to_all x1 -> x0, starting transfers between devices: 9.51 us -> none  [reduce_pieces(): parts = lax.all_to_all(chip, ('x', 'zl', 'zh'), 0, 0)]
    ppermute x8 -> x14, waiting for transfers between devices: 19 us -> 26.9 us  [moved(): return lax.ppermute(value, AXES, pairs)]
    pallas_call x1, Pallas kernels: 28.4 us -> 25.1 us  [attention(): pl.pallas_call(attention_kernel, grid_spec=pltpu.PrefetchScalarGridSpec(n...]
  transfers between devices with their start and end apart: 16 -> 21, of which waited for: 8 -> 10; matrix products, arithmetic and copies ran while one was open for 2% -> 2% of each run, Pallas kernels for 0% -> 0%
where the time goes in v3:
time: 94.6 us; the launch traced here: 93.7 us
  starting transfers between devices  32.7 us (35%)
  waiting for transfers between devices  29.2 us (31%)
  Pallas kernels  25.1 us (27%)
  other arithmetic  3.77 us (4%)
  local copies, waits for them, and re-layouts  1.98 us (2%)
  between operations  0.96 us (1%)
    ppermute x14, starting transfers between devices, moved(): return lax.ppermute(value, AXES, pairs)  31.7 us
    ppermute x14, waiting for transfers between devices, moved(): return lax.ppermute(value, AXES, pairs)  26.9 us
    pallas_call x1, Pallas kernels, attention(): pl.pallas_call(attention_kernel, grid_spec=pltpu.PrefetchScalarGridSpec(n...  25.1 us
    ppermute x7, waiting for transfers between devices, swap_cores(): return lax.ppermute(value, 'core', [(0, 1), (1, 0)])  2.31 us
  transfers between devices with their start and end apart: 21, of which 10 were waited for; matrix products, arithmetic and copies ran while one was open for 2% of the time, Pallas kernels for 0%

profile of v3, /device:TPU:4, one launch (start us, length us, event | category | flops | bytes accessed | tf_op | source)
XLA Modules:
  0.0 93.7 jit_solution(14784617572891119585)
XLA Ops:
  0.7 1.8 %maximum_select_fusion = bf16[3,192,1024]{2,1,0:T(8,128)(2,1)S(1)} fusion(bf16[1,192,1024]{2,1,0:T(8,128)(2,1)} %bitcast.56, bf16[1,192,1024]{2,1,0:T(8,128)(2,1)} %bitcast.54, bf16[1,192,1024]{2,1,0:T(8,128)(2,1)} %bitcast.52, bf16[1,192,1024]{2,1,0:T(8,128)(2,1)} %bitcast.55, bf16[1,192,1024]{2,1,0:T(8,128)(2,1)} %bitcast.53, ...), kind=kLoop, calls=%fused_computation.1 | loop fusion | flops 2949120 | bytes 3538945 | tf_op jit(solution)/shard_map/jit(_where)/select_n | solution.py:332
  2.6 3.9 %collective-permute-start.3 = (bf16[2,32,384]{2,1,0:T(8,128)(2,1)S(1)}, bf16[2,32,384]{2,1,0:T(8,128)(2,1)S(1)}, u32[]{:S(2)}, u32[]{:S(2)}) collective-permute-start(bf16[2,32,384]{2,1,0:T(8,128)(2,1)S(1)} %pad_maximum_fusion.1), channel_id=1, source_target_pairs={{0,96},{2,0},{4,32},{6,64},{8,104},{10,8},{12,40},{14,72},{16,112}... | collective-permute-start | bytes 147464 | tf_op jit(solution)/shard_map/ppermute | solution.py:289
  6.5 2.5 %collective-permute-start = (bf16[2,32,384]{2,1,0:T(8,128)(2,1)S(1)}, bf16[2,32,384]{2,1,0:T(8,128)(2,1)S(1)}, u32[]{:S(2)}, u32[]{:S(2)}) collective-permute-start(bf16[2,32,384]{2,1,0:T(8,128)(2,1)S(1)} %pad_maximum_fusion.1), channel_id=1, source_target_pairs={{0,0},{2,32},{4,64},{6,96},{8,8},{10,40},{12,72},{14,104},{16,16},... | collective-permute-start | bytes 147464 | tf_op jit(solution)/shard_map/ppermute | solution.py:289
  9.0 1.7 %collective-permute-start.1 = (bf16[2,32,384]{2,1,0:T(8,128)(2,1)S(1)}, bf16[2,32,384]{2,1,0:T(8,128)(2,1)S(1)}, u32[]{:S(2)}, u32[]{:S(2)}) collective-permute-start(bf16[2,32,384]{2,1,0:T(8,128)(2,1)S(1)} %pad_maximum_fusion.1), channel_id=1, source_target_pairs={{0,32},{2,64},{4,96},{6,0},{8,40},{10,72},{12,104},{14,8},{16,48},... | collective-permute-start | bytes 147464 | tf_op jit(solution)/shard_map/ppermute | solution.py:289
  11.4 5.0 %collective-permute-done = bf16[2,32,384]{2,1,0:T(8,128)(2,1)S(1)} collective-permute-done((bf16[2,32,384]{2,1,0:T(8,128)(2,1)S(1)}, bf16[2,32,384]{2,1,0:T(8,128)(2,1)S(1)}, u32[]{:S(2)}, u32[]{:S(2)}) %collective-permute-start) | collective-permute-done | bytes 49184 | tf_op jit(solution)/shard_map/ppermute | solution.py:289
  16.5 4.0 %collective-permute-start.6 = (bf16[4,2,32,384]{3,2,1,0:T(8,128)(2,1)S(1)}, bf16[4,2,32,384]{3,2,1,0:T(8,128)(2,1)S(1)}, u32[]{:S(2)}, u32[]{:S(2)}) collective-permute-start(bf16[4,2,32,384]{3,2,1,0:T(8,128)(2,1)S(1)} %pad_maximum_fusion.refs_0_), channel_id=1, source_target_pairs={{0,1},{2,3},{4,5},{6,7},{8,9},{10,11},{12,13},{14,15},{16,17},{18,... | collective-permute-start | bytes 589832 | tf_op jit(solution)/shard_map/ppermute | solution.py:289
  20.4 0.7 collective-permute-start.7
  21.1 1.3 %collective-permute-start.5 = (bf16[4,2,32,384]{3,2,1,0:T(8,128)(2,1)S(1)}, bf16[4,2,32,384]{3,2,1,0:T(8,128)(2,1)S(1)}, u32[]{:S(2)}, u32[]{:S(2)}) collective-permute-start(bf16[4,2,32,384]{3,2,1,0:T(8,128)(2,1)S(1)} %pad_maximum_fusion.refs_0_), channel_id=1, source_target_pairs={{0,16},{2,18},{4,20},{6,22},{8,24},{10,26},{12,28},{14,30},{16,1},... | collective-permute-start | bytes 589832 | tf_op jit(solution)/shard_map/ppermute | solution.py:289
  22.5 3.8 %collective-permute-done.6.refs_2_ = bf16[4,2,32,384]{3,2,1,0:T(8,128)(2,1)S(1)} collective-permute-done((bf16[4,2,32,384]{3,2,1,0:T(8,128)(2,1)S(1)}, bf16[4,2,32,384]{3,2,1,0:T(8,128)(2,1)S(1)}, u32[]{:S(2)}, u32[]{:S(2)}) %collective-permute-start.6) | collective-permute-done | bytes 196640 | tf_op jit(solution)/shard_map/ppermute | solution.py:289
  26.3 3.3 %collective-permute-done.7.refs_3_ = bf16[4,2,32,384]{3,2,1,0:T(8,128)(2,1)S(1)} collective-permute-done((bf16[4,2,32,384]{3,2,1,0:T(8,128)(2,1)S(1)}, bf16[4,2,32,384]{3,2,1,0:T(8,128)(2,1)S(1)}, u32[]{:S(2)}, u32[]{:S(2)}) %collective-permute-start.7) | collective-permute-done | bytes 196640 | tf_op jit(solution)/shard_map/ppermute | solution.py:289
  31.4 0.7 copy-done.8
  32.1 25.1 %attention.1 = (bf16[192,1024]{1,0:T(8,128)(2,1)}, bf16[192,1024]{1,0:T(8,128)(2,1)}, bf16[16,2,32,384]{3,2,1,0:T(8,128)(2,1)S(1)}, bf16[16,2,32,384]{3,2,1,0:T(8,128)(2,1)S(1)}) custom-call(s32[48]{0:T(128)} %order_ref.1, s32[3]{0:T(128)} %pad_add_fusion.place_ref, bf16[4,2,32,384]{3,2,1,0:T(8,128)(2,1)} %copy-done.1, bf16[4,2,32,384]{3,2,1,0:T(8,128)(2,1)} %copy-done.5, ...), custom_call_target="tpu_custom_call" | custom-call | tf_op jit(solution)/shard_map/attention/pallas_call | solution.py:237
  57.6 2.0 %collective-permute-done.13 = bf16[16,2,32,384]{3,2,1,0:T(8,128)(2,1)S(1)} collective-permute-done((bf16[16,2,32,384]{3,2,1,0:T(8,128)(2,1)S(1)}, bf16[16,2,32,384]{3,2,1,0:T(8,128)(2,1)S(1)}, u32[]{:S(2)}, u32[]{:S(2)}) %collective-permute-start.13) | collective-permute-done | bytes 786464 | tf_op jit(solution)/shard_map/ppermute | solution.py:293
  60.1 1.8 %collective-permute-start.14 = (bf16[4,2,32,384]{3,2,1,0:T(8,128)(2,1)S(1)}, bf16[4,2,32,384]{3,2,1,0:T(8,128)(2,1)S(1)}, u32[]{:S(2)}, u32[]{:S(2)}) collective-permute-start(bf16[4,2,32,384]{3,2,1,0:T(8,128)(2,1)S(1)} %get-tuple-element.16), channel_id=1, source_target_pairs={{0,16},{2,18},{4,20},{6,22},{8,24},{10,26},{12,28},{14,30},{16,1},... | collective-permute-start | bytes 589832 | tf_op jit(solution)/shard_map/ppermute | solution.py:289
  61.8 3.5 %collective-permute-start.15 = (bf16[4,2,32,384]{3,2,1,0:T(8,128)(2,1)S(1)}, bf16[4,2,32,384]{3,2,1,0:T(8,128)(2,1)S(1)}, u32[]{:S(2)}, u32[]{:S(2)}) collective-permute-start(bf16[4,2,32,384]{3,2,1,0:T(8,128)(2,1)S(1)} %get-tuple-element.18), channel_id=1, source_target_pairs={{0,1},{2,3},{4,5},{6,7},{8,9},{10,11},{12,13},{14,15},{16,17},{18,... | collective-permute-start | bytes 589832 | tf_op jit(solution)/shard_map/ppermute | solution.py:289
  65.4 3.8 %collective-permute-done.14 = bf16[4,2,32,384]{3,2,1,0:T(8,128)(2,1)S(1)} collective-permute-done((bf16[4,2,32,384]{3,2,1,0:T(8,128)(2,1)S(1)}, bf16[4,2,32,384]{3,2,1,0:T(8,128)(2,1)S(1)}, u32[]{:S(2)}, u32[]{:S(2)}) %collective-permute-start.14) | collective-permute-done | bytes 196640 | tf_op jit(solution)/shard_map/ppermute | solution.py:289
  69.2 5.4 %collective-permute-done.15 = bf16[4,2,32,384]{3,2,1,0:T(8,128)(2,1)S(1)} collective-permute-done((bf16[4,2,32,384]{3,2,1,0:T(8,128)(2,1)S(1)}, bf16[4,2,32,384]{3,2,1,0:T(8,128)(2,1)S(1)}, u32[]{:S(2)}, u32[]{:S(2)}) %collective-permute-start.15) | collective-permute-done | bytes 196640 | tf_op jit(solution)/shard_map/ppermute | solution.py:289
  74.7 6.5 %collective-permute-start.17 = (bf16[2,32,384]{2,1,0:T(8,128)(2,1)S(1)}, bf16[2,32,384]{2,1,0:T(8,128)(2,1)S(1)}, u32[]{:S(2)}, u32[]{:S(2)}) collective-permute-start(bf16[2,32,384]{2,1,0:T(8,128)(2,1)S(1)} %get-tuple-element.21), channel_id=1, source_target_pairs={{0,0},{2,32},{4,64},{6,96},{8,8},{10,40},{12,72},{14,104},{16,16},... | collective-permute-start | bytes 147464 | tf_op jit(solution)/shard_map/ppermute | solution.py:289
  81.2 5.3 %collective-permute-start.18 = (bf16[2,32,384]{2,1,0:T(8,128)(2,1)S(1)}, bf16[2,32,384]{2,1,0:T(8,128)(2,1)S(1)}, u32[]{:S(2)}, u32[]{:S(2)}) collective-permute-start(bf16[2,32,384]{2,1,0:T(8,128)(2,1)S(1)} %get-tuple-element.24), channel_id=1, source_target_pairs={{0,2},{2,34},{4,66},{6,98},{8,10},{10,42},{12,74},{14,106},{16,18}... | collective-permute-start | bytes 147464 | tf_op jit(solution)/shard_map/ppermute | solution.py:289
  86.5 0.9 broadcast_select_fusion
  87.5 0.8 collective-permute-done.18
  88.3 3.8 %collective-permute-done.19 = bf16[2,32,384]{2,1,0:T(8,128)(2,1)S(1)} collective-permute-done((bf16[2,32,384]{2,1,0:T(8,128)(2,1)S(1)}, bf16[2,32,384]{2,1,0:T(8,128)(2,1)S(1)}, u32[]{:S(2)}, u32[]{:S(2)}) %collective-permute-start.19) | collective-permute-done | bytes 49184 | tf_op jit(solution)/shard_map/ppermute | solution.py:289
  92.1 0.9 collective-permute-done.20
  93.1 0.6 slice_bitcast_fusion
  (55 shorter events, 3.6 us)
Async XLA Ops:
  2.5 14.0 %collective-permute-start.4 = (bf16[3,192,1024]{2,1,0:T(8,128)(2,1)S(1)}, bf16[3,192,1024]{2,1,0:T(8,128)(2,1)S(1)}, u32[]{:S(2)}, u32[]{:S(2)}) collective-permute-start(bf16[3,192,1024]{2,1,0:T(8,128)(2,1)S(1)} %maximum_select_fusion), channel_id=1, source_target_pairs={{0,8},{8,0},{1,9},{9,1},{2,10},{10,2},{3,11},{11,3},{4,12},{12,4},... | collective-permute-start | bytes 3538952 | tf_op jit(solution)/shard_map/ppermute | solution.py:293
  2.6 8.7 %collective-permute-start.3 = (bf16[2,32,384]{2,1,0:T(8,128)(2,1)S(1)}, bf16[2,32,384]{2,1,0:T(8,128)(2,1)S(1)}, u32[]{:S(2)}, u32[]{:S(2)}) collective-permute-start(bf16[2,32,384]{2,1,0:T(8,128)(2,1)S(1)} %pad_maximum_fusion.1), channel_id=1, source_target_pairs={{0,96},{2,0},{4,32},{6,64},{8,104},{10,8},{12,40},{14,72},{16,112}... | collective-permute-start | bytes 147464 | tf_op jit(solution)/shard_map/ppermute | solution.py:289
  6.5 9.9 %collective-permute-start = (bf16[2,32,384]{2,1,0:T(8,128)(2,1)S(1)}, bf16[2,32,384]{2,1,0:T(8,128)(2,1)S(1)}, u32[]{:S(2)}, u32[]{:S(2)}) collective-permute-start(bf16[2,32,384]{2,1,0:T(8,128)(2,1)S(1)} %pad_maximum_fusion.1), channel_id=1, source_target_pairs={{0,0},{2,32},{4,64},{6,96},{8,8},{10,40},{12,72},{14,104},{16,16},... | collective-permute-start | bytes 147464 | tf_op jit(solution)/shard_map/ppermute | solution.py:289
  9.0 7.4 %collective-permute-start.1 = (bf16[2,32,384]{2,1,0:T(8,128)(2,1)S(1)}, bf16[2,32,384]{2,1,0:T(8,128)(2,1)S(1)}, u32[]{:S(2)}, u32[]{:S(2)}) collective-permute-start(bf16[2,32,384]{2,1,0:T(8,128)(2,1)S(1)} %pad_maximum_fusion.1), channel_id=1, source_target_pairs={{0,32},{2,64},{4,96},{6,0},{8,40},{10,72},{12,104},{14,8},{16,48},... | collective-permute-start | bytes 147464 | tf_op jit(solution)/shard_map/ppermute | solution.py:289
  10.7 5.7 %collective-permute-start.2 = (bf16[2,32,384]{2,1,0:T(8,128)(2,1)S(1)}, bf16[2,32,384]{2,1,0:T(8,128)(2,1)S(1)}, u32[]{:S(2)}, u32[]{:S(2)}) collective-permute-start(bf16[2,32,384]{2,1,0:T(8,128)(2,1)S(1)} %pad_maximum_fusion.1), channel_id=1, source_target_pairs={{0,64},{2,96},{4,0},{6,32},{8,72},{10,104},{12,8},{14,40},{16,80},... | collective-permute-start | bytes 147464 | tf_op jit(solution)/shard_map/ppermute | solution.py:289
  16.4 15.7 %copy-start.1 = (bf16[4,2,32,384]{3,2,1,0:T(8,128)(2,1)}, bf16[4,2,32,384]{3,2,1,0:T(8,128)(2,1)S(1)}, u32[]{:S(2)}) copy-start(bf16[4,2,32,384]{3,2,1,0:T(8,128)(2,1)S(1)} %pad_maximum_fusion.refs_0_) | copy-start | bytes 589828
  16.5 15.6 %copy-start = (bf16[3,192,1024]{2,1,0:T(8,128)(2,1)}, bf16[3,192,1024]{2,1,0:T(8,128)(2,1)S(1)}, u32[]{:S(2)}) copy-start(bf16[3,192,1024]{2,1,0:T(8,128)(2,1)S(1)} %collective-permute-done.4.refs_14_) | copy-start | bytes 3538948
  16.5 9.8 %collective-permute-start.6 = (bf16[4,2,32,384]{3,2,1,0:T(8,128)(2,1)S(1)}, bf16[4,2,32,384]{3,2,1,0:T(8,128)(2,1)S(1)}, u32[]{:S(2)}, u32[]{:S(2)}) collective-permute-start(bf16[4,2,32,384]{3,2,1,0:T(8,128)(2,1)S(1)} %pad_maximum_fusion.refs_0_), channel_id=1, source_target_pairs={{0,1},{2,3},{4,5},{6,7},{8,9},{10,11},{12,13},{14,15},{16,17},{18,... | collective-permute-start | bytes 589832 | tf_op jit(solution)/shard_map/ppermute | solution.py:289
  20.4 9.1 %collective-permute-start.7 = (bf16[4,2,32,384]{3,2,1,0:T(8,128)(2,1)S(1)}, bf16[4,2,32,384]{3,2,1,0:T(8,128)(2,1)S(1)}, u32[]{:S(2)}, u32[]{:S(2)}) collective-permute-start(bf16[4,2,32,384]{3,2,1,0:T(8,128)(2,1)S(1)} %pad_maximum_fusion.refs_0_), channel_id=1, source_target_pairs={{0,17},{2,19},{4,21},{6,23},{8,25},{10,27},{12,29},{14,31},{16,0},... | collective-permute-start | bytes 589832 | tf_op jit(solution)/shard_map/ppermute | solution.py:289
  21.1 8.4 %collective-permute-start.5 = (bf16[4,2,32,384]{3,2,1,0:T(8,128)(2,1)S(1)}, bf16[4,2,32,384]{3,2,1,0:T(8,128)(2,1)S(1)}, u32[]{:S(2)}, u32[]{:S(2)}) collective-permute-start(bf16[4,2,32,384]{3,2,1,0:T(8,128)(2,1)S(1)} %pad_maximum_fusion.refs_0_), channel_id=1, source_target_pairs={{0,16},{2,18},{4,20},{6,22},{8,24},{10,26},{12,28},{14,30},{16,1},... | collective-permute-start | bytes 589832 | tf_op jit(solution)/shard_map/ppermute | solution.py:289
  22.5 8.2 %collective-permute-start.8 = (bf16[4,2,32,384]{3,2,1,0:T(8,128)(2,1)S(1)}, bf16[4,2,32,384]{3,2,1,0:T(8,128)(2,1)S(1)}, u32[]{:S(2)}, u32[]{:S(2)}) collective-permute-start(bf16[4,2,32,384]{3,2,1,0:T(8,128)(2,1)S(1)} %pad_maximum_fusion.refs_0_), channel_id=1, source_target_pairs={{0,8},{8,0},{1,9},{9,1},{2,10},{10,2},{3,11},{11,3},{4,12},{12,4},... | collective-permute-start | bytes 589832 | tf_op jit(solution)/shard_map/ppermute | solution.py:293
  26.3 4.4 %collective-permute-start.10 = (bf16[4,2,32,384]{3,2,1,0:T(8,128)(2,1)S(1)}, bf16[4,2,32,384]{3,2,1,0:T(8,128)(2,1)S(1)}, u32[]{:S(2)}, u32[]{:S(2)}) collective-permute-start(bf16[4,2,32,384]{3,2,1,0:T(8,128)(2,1)S(1)} %collective-permute-done.6.refs_2_), channel_id=1, source_target_pairs={{0,8},{8,0},{1,9},{9,1},{2,10},{10,2},{3,11},{11,3},{4,12},{12,4},... | collective-permute-start | bytes 589832 | tf_op jit(solution)/shard_map/ppermute | solution.py:293
  29.5 1.4 %collective-permute-start.11 = (bf16[4,2,32,384]{3,2,1,0:T(8,128)(2,1)S(1)}, bf16[4,2,32,384]{3,2,1,0:T(8,128)(2,1)S(1)}, u32[]{:S(2)}, u32[]{:S(2)}) collective-permute-start(bf16[4,2,32,384]{3,2,1,0:T(8,128)(2,1)S(1)} %collective-permute-done.7.refs_3_), channel_id=1, source_target_pairs={{0,8},{8,0},{1,9},{9,1},{2,10},{10,2},{3,11},{11,3},{4,12},{12,4},... | collective-permute-start | bytes 589832 | tf_op jit(solution)/shard_map/ppermute | solution.py:293
  29.6 2.5 %collective-permute-start.9 = (bf16[4,2,32,384]{3,2,1,0:T(8,128)(2,1)S(1)}, bf16[4,2,32,384]{3,2,1,0:T(8,128)(2,1)}, u32[]{:S(2)}, u32[]{:S(2)}) collective-permute-start(bf16[4,2,32,384]{3,2,1,0:T(8,128)(2,1)S(1)} %collective-permute-done.5.refs_1_), channel_id=1, source_target_pairs={{0,8},{8,0},{1,9},{9,1},{2,10},{10,2},{3,11},{11,3},{4,12},{12,4},... | collective-permute-start | bytes 589832 | tf_op jit(solution)/shard_map/ppermute | solution.py:293
  57.3 2.4 %collective-permute-start.13 = (bf16[16,2,32,384]{3,2,1,0:T(8,128)(2,1)S(1)}, bf16[16,2,32,384]{3,2,1,0:T(8,128)(2,1)S(1)}, u32[]{:S(2)}, u32[]{:S(2)}) collective-permute-start(bf16[16,2,32,384]{3,2,1,0:T(8,128)(2,1)S(1)} %get-tuple-element.15), channel_id=1, source_target_pairs={{0,8},{8,0},{1,9},{9,1},{2,10},{10,2},{3,11},{11,3},{4,12},{12,4},... | collective-permute-start | bytes 2359304 | tf_op jit(solution)/shard_map/ppermute | solution.py:293
  60.0 26.6 %copy-start.2 = (bf16[192,1024]{1,0:T(8,128)(2,1)S(1)}, bf16[192,1024]{1,0:T(8,128)(2,1)}, u32[]{:S(2)}) copy-start(bf16[192,1024]{1,0:T(8,128)(2,1)} %get-tuple-element.12) | copy-start | bytes 1179652
  60.1 9.1 %collective-permute-start.14 = (bf16[4,2,32,384]{3,2,1,0:T(8,128)(2,1)S(1)}, bf16[4,2,32,384]{3,2,1,0:T(8,128)(2,1)S(1)}, u32[]{:S(2)}, u32[]{:S(2)}) collective-permute-start(bf16[4,2,32,384]{3,2,1,0:T(8,128)(2,1)S(1)} %get-tuple-element.16), channel_id=1, source_target_pairs={{0,16},{2,18},{4,20},{6,22},{8,24},{10,26},{12,28},{14,30},{16,1},... | collective-permute-start | bytes 589832 | tf_op jit(solution)/shard_map/ppermute | solution.py:289
  61.8 12.7 %collective-permute-start.15 = (bf16[4,2,32,384]{3,2,1,0:T(8,128)(2,1)S(1)}, bf16[4,2,32,384]{3,2,1,0:T(8,128)(2,1)S(1)}, u32[]{:S(2)}, u32[]{:S(2)}) collective-permute-start(bf16[4,2,32,384]{3,2,1,0:T(8,128)(2,1)S(1)} %get-tuple-element.18), channel_id=1, source_target_pairs={{0,1},{2,3},{4,5},{6,7},{8,9},{10,11},{12,13},{14,15},{16,17},{18,... | collective-permute-start | bytes 589832 | tf_op jit(solution)/shard_map/ppermute | solution.py:289
  65.3 9.3 %collective-permute-start.16 = (bf16[4,2,32,384]{3,2,1,0:T(8,128)(2,1)S(1)}, bf16[4,2,32,384]{3,2,1,0:T(8,128)(2,1)S(1)}, u32[]{:S(2)}, u32[]{:S(2)}) collective-permute-start(bf16[4,2,32,384]{3,2,1,0:T(8,128)(2,1)S(1)} %get-tuple-element.17), channel_id=1, source_target_pairs={{0,17},{2,19},{4,21},{6,23},{8,25},{10,27},{12,29},{14,31},{16,0},... | collective-permute-start | bytes 589832 | tf_op jit(solution)/shard_map/ppermute | solution.py:289
  65.3 21.2 %collective-permute-start.12 = (bf16[192,1024]{1,0:T(8,128)(2,1)S(1)}, bf16[192,1024]{1,0:T(8,128)(2,1)S(1)}, u32[]{:S(2)}, u32[]{:S(2)}) collective-permute-start(bf16[192,1024]{1,0:T(8,128)(2,1)S(1)} %copy-done.11), channel_id=1, source_target_pairs={{0,8},{8,0},{1,9},{9,1},{2,10},{10,2},{3,11},{11,3},{4,12},{12,4},... | collective-permute-start | bytes 1179656 | tf_op jit(solution)/shard_map/ppermute | solution.py:293
  74.7 12.8 %collective-permute-start.17 = (bf16[2,32,384]{2,1,0:T(8,128)(2,1)S(1)}, bf16[2,32,384]{2,1,0:T(8,128)(2,1)S(1)}, u32[]{:S(2)}, u32[]{:S(2)}) collective-permute-start(bf16[2,32,384]{2,1,0:T(8,128)(2,1)S(1)} %get-tuple-element.21), channel_id=1, source_target_pairs={{0,0},{2,32},{4,64},{6,96},{8,8},{10,40},{12,72},{14,104},{16,16},... | collective-permute-start | bytes 147464 | tf_op jit(solution)/shard_map/ppermute | solution.py:289
  81.2 7.1 %collective-permute-start.18 = (bf16[2,32,384]{2,1,0:T(8,128)(2,1)S(1)}, bf16[2,32,384]{2,1,0:T(8,128)(2,1)S(1)}, u32[]{:S(2)}, u32[]{:S(2)}) collective-permute-start(bf16[2,32,384]{2,1,0:T(8,128)(2,1)S(1)} %get-tuple-element.24), channel_id=1, source_target_pairs={{0,2},{2,34},{4,66},{6,98},{8,10},{10,42},{12,74},{14,106},{16,18}... | collective-permute-start | bytes 147464 | tf_op jit(solution)/shard_map/ppermute | solution.py:289
  86.5 5.6 %collective-permute-start.19 = (bf16[2,32,384]{2,1,0:T(8,128)(2,1)S(1)}, bf16[2,32,384]{2,1,0:T(8,128)(2,1)S(1)}, u32[]{:S(2)}, u32[]{:S(2)}) collective-permute-start(bf16[2,32,384]{2,1,0:T(8,128)(2,1)S(1)} %get-tuple-element.23), channel_id=1, source_target_pairs={{0,4},{2,36},{4,68},{6,100},{8,12},{10,44},{12,76},{14,108},{16,20... | collective-permute-start | bytes 147464 | tf_op jit(solution)/shard_map/ppermute | solution.py:289
  86.5 6.5 %collective-permute-start.20 = (bf16[2,32,384]{2,1,0:T(8,128)(2,1)S(1)}, bf16[2,32,384]{2,1,0:T(8,128)(2,1)S(1)}, u32[]{:S(2)}, u32[]{:S(2)}) collective-permute-start(bf16[2,32,384]{2,1,0:T(8,128)(2,1)S(1)} %get-tuple-element.22), channel_id=1, source_target_pairs={{0,6},{2,38},{4,70},{6,102},{8,14},{10,46},{12,78},{14,110},{16,22... | collective-permute-start | bytes 147464 | tf_op jit(solution)/shard_map/ppermute | solution.py:289
  (9 other events, 22.5 us)
